TPU v7x, 256 devices: a whole 4x4x8 slice. The times are simulated.
256 devices in a mesh: fine: 8 (over z_hi, core), coarse: 32 (over x, y, z_lo).
Axes of the slice: x: 4, y: 4, z: 8 (z_hi: 4, z_lo: 2; z = z_hi * 2 + z_lo), core: 2. Of those that a mesh axis runs over, the one named last changes fastest.
Arguments:
- query_rows: bfloat16 [32, 8, 128, 3072], P('coarse', 'fine'), may hold values from -5 to 5
- key_rows: bfloat16 [32, 8, 128, 3072], P('coarse', 'fine'), may hold values from -5 to 5
- value_rows: bfloat16 [32, 8, 128, 3072], P('coarse', 'fine'), may hold values from -5 to 5
- out_grad: bfloat16 [32, 8, 128, 3072], P('coarse', 'fine'), may hold values from -5 to 5
Outputs:
- attended: bfloat16 [32, 8, 128, 3072], P('coarse', 'fine')
- query_grad: bfloat16 [32, 8, 128, 3072], P('coarse', 'fine')
- key_grad: bfloat16 [32, 8, 128, 3072], P('coarse', 'fine')
- value_grad: bfloat16 [32, 8, 128, 3072], P('coarse', 'fine')
All inputs are finite; a program needn't handle non-finite values.
Results may differ from a plain program's by a relative error of at most 0.0079.
Values may be sent and summed in bfloat16 or wider, within the bound.
No kernel may reach another device: no remote copies, remote signals or barrier semaphores. Data moves between devices by JAX's collectives and lax.ppermute only.
A program may use at most 128 MiB of HBM per device.

v0:
```python
import functools
import math

import jax
import jax.numpy as jnp
from jax import lax
from jax.experimental import pallas as pl
from jax.experimental.pallas import tpu as pltpu
from jax.sharding import PartitionSpec as P

HEADS = 24
HEAD_DIM = 128
ROWS = 128
BLOCK = 256
CORE_HEADS = HEADS // 2
HALF = CORE_HEADS * HEAD_DIM
SCALE = HEAD_DIM**-0.5
EXP2_SCALE = SCALE * math.log2(math.e)
COST = pl.CostEstimate(flops=1, bytes_accessed=1, transcendentals=0)
CHUNKS = (3, 3, 3, 3)
PARITY = (0, 0, 0, 1)
ORDER = (
    "K0", "Q0", "A0", "B1", "B2", "D1", "B3", "B0", "D2", "E1",
    "D3", "E2", "D0", "F1", "E3", "E0", "G1", "S0", "F3", "R0",
    "F2", "F0", "G2", "H1", "G0", "H2", "G3", "H0", "T0", "H3",
)
VMEM_LIMIT = 40 * 2**20
BF16 = jnp.bfloat16
F32 = jnp.float32
ANYWHERE = pl.BlockSpec(memory_space=pl.ANY)


def params(steps=1):
    return pltpu.CompilerParams(
        dimension_semantics=("arbitrary",) * steps, vmem_limit_bytes=VMEM_LIMIT
    )


def averager(rows, group):
    row = lax.broadcasted_iota(jnp.int32, (rows, rows * group), 0)
    col = lax.broadcasted_iota(jnp.int32, (rows, rows * group), 1)
    return jnp.where(col // group == row, 1.0 / group, 0.0).astype(BF16)


def spreader(rows, group):
    row = lax.broadcasted_iota(jnp.int32, (rows * group, rows), 0)
    col = lax.broadcasted_iota(jnp.int32, (rows * group, rows), 1)
    return jnp.where(row // group == col, 1.0 / group, 0.0).astype(BF16)


def dot(a, b, dims=((1,), (0,))):
    return lax.dot_general(a, b, (dims, ((), ())), preferred_element_type=F32)


def extract_kernel(core, a_ref, b_ref, *refs):
    out_ref = refs[-1]
    out_ref[0] = a_ref[...]
    out_ref[1] = b_ref[...]


def extract_other(core, a, b, after, limit):
    half = pl.BlockSpec((ROWS, HALF), lambda i, c: (0, 1 - c[0]))
    return pl.pallas_call(
        extract_kernel,
        grid_spec=pltpu.PrefetchScalarGridSpec(
            num_scalar_prefetch=1,
            grid=(1,),
            in_specs=[half, half] + [ANYWHERE] * len(after),
            out_specs=pl.BlockSpec((2, ROWS, HALF), lambda i, c: (0, 0, 0)),
        ),
        out_shape=jax.ShapeDtypeStruct((2, ROWS, HALF), BF16),
        cost_estimate=COST,
        compiler_params=pltpu.CompilerParams(vmem_limit_bytes=limit),
        name="extract_other",
    )(core, a, b, *after)


def pack_first_kernel(core, k_ref, v_ref, kv_ref, *refs):
    outs = refs[-2 * len(CHUNKS) :]
    weights = jnp.concatenate(
        [averager(BLOCK >> level, 1 << level) for level in (1, 2, 3)], axis=0
    )
    for part, own in enumerate((k_ref, v_ref)):
        rows = jnp.concatenate([own[...], kv_ref[part]], axis=0)
        lane = 0
        for number, heads in enumerate(CHUNKS):
            width = heads * HEAD_DIM
            coarse = dot(weights, rows[:, lane : lane + width]).astype(BF16)
            outs[2 * number][part] = coarse[:128]
            outs[2 * number + 1][part] = coarse[128:]
            lane += width


def pack_first(core, keys, values, kv_recv, after):
    half = pl.BlockSpec((ROWS, HALF), lambda i, c: (0, c[0]))
    whole = pl.BlockSpec((2, ROWS, HALF), lambda i, c: (0, 0, 0))
    shapes = [(2, count, heads * HEAD_DIM) for heads in CHUNKS for count in (128, 96)]
    return pl.pallas_call(
        pack_first_kernel,
        grid_spec=pltpu.PrefetchScalarGridSpec(
            num_scalar_prefetch=1,
            grid=(1,),
            in_specs=[half, half, whole] + [ANYWHERE] * len(after),
            out_specs=[pl.BlockSpec(shape, lambda i, c: (0, 0, 0)) for shape in shapes],
        ),
        out_shape=[jax.ShapeDtypeStruct(shape, BF16) for shape in shapes],
        cost_estimate=COST,
        compiler_params=params(),
        name="pack_first",
    )(core, keys, values, kv_recv, *after)


def whole_call(kernel, name, out_shape, after, *args):
    return pl.pallas_call(
        kernel,
        in_specs=[pl.BlockSpec(memory_space=pltpu.VMEM)] * len(args) + [ANYWHERE] * len(after),
        out_specs=pl.BlockSpec(memory_space=pltpu.VMEM),
        out_shape=out_shape,
        cost_estimate=COST,
        compiler_params=pltpu.CompilerParams(vmem_limit_bytes=VMEM_LIMIT),
        name=name,
    )(*args, *after)


def pack_second_kernel(own_ref, first_ref, *refs):
    out_ref = refs[-1]
    pairs = averager(64, 2)
    for part in range(2):
        out_ref[part, :64] = own_ref[part, :64]
        out_ref[part, 64:] = dot(pairs, first_ref[part]).astype(BF16)


def pack_third_kernel(own_ref, first_ref, second_ref, *refs):
    out_ref = refs[-1]
    fours = averager(32, 4)
    pairs = averager(64, 2)
    for part in range(2):
        out_ref[part, :32] = own_ref[part, 64:]
        out_ref[part, 32:64] = dot(fours, first_ref[part]).astype(BF16)
        out_ref[part, 64:] = dot(pairs, second_ref[part]).astype(BF16)


def attend_kernel(start, heads, core, q_own, g_own, k_own, v_own, *refs):
    for head in range(heads):
        attend_head(start, head, core, q_own, g_own, k_own, v_own, *refs)


def attend_head(
    start, head, core, q_own, g_own, k_own, v_own, qg_recv, kv_recv, first, second, third, *refs
):
    own_out, peer_out, exact_out, first_out, second_out, third_out = refs[-6:]
    own = pl.ds(pl.multiple_of(core[0] * HALF + (start + head) * HEAD_DIM, HEAD_DIM), HEAD_DIM)
    recv = pl.ds((start + head) * HEAD_DIM, HEAD_DIM)
    local = pl.ds(head * HEAD_DIM, HEAD_DIM)
    queries = jnp.concatenate([q_own[:, own], qg_recv[0, :, recv]], axis=0)
    grads = jnp.concatenate([g_own[:, own], qg_recv[1, :, recv]], axis=0)
    keys, values = (
        jnp.concatenate(
            [mine[:, own], kv_recv[part, :, recv]]
            + [rows[part, :, local] for rows in (first, second, third)],
            axis=0,
        )
        for part, mine in enumerate((k_own, v_own))
    )
    scores = dot(keys, queries, ((1,), (1,)))
    prob_grad = dot(values, grads, ((1,), (1,)))
    pieces = [slice(low, low + ROWS) for low in range(0, 5 * ROWS, ROWS)]

    def fold(block):
        return block.reshape(ROWS // 8, 8, BLOCK)

    tops = [jnp.max(fold(scores[piece]), axis=0) for piece in pieces]
    row_max = jnp.max(functools.reduce(jnp.maximum, tops), axis=0, keepdims=True)
    exp_scores, exp_sum, exp_grad = [], 0.0, 0.0
    for piece in pieces:
        block = jnp.exp2((scores[piece] - row_max) * EXP2_SCALE)
        exp_scores.append(block)
        exp_sum += jnp.sum(fold(block), axis=0)
        exp_grad += jnp.sum(fold(block * prob_grad[piece]), axis=0)
    inverse = 1.0 / jnp.sum(exp_sum, axis=0, keepdims=True)
    row_inner = jnp.sum(exp_grad, axis=0, keepdims=True) * inverse
    weights_low, score_grad = [], []
    for piece, block in zip(pieces, exp_scores):
        weights = block * inverse
        weights_low.append(weights.astype(BF16))
        score_grad.append((weights * (prob_grad[piece] - row_inner)).astype(BF16))
    weights_low = jnp.concatenate(weights_low, axis=0)
    score_grad = jnp.concatenate(score_grad, axis=0)
    attended = dot(values.T, weights_low).T
    query_grad = dot(keys.T, score_grad).T * SCALE
    for part, result in enumerate((attended, query_grad)):
        result = result.astype(BF16)
        own_out[part, :, recv] = result[:ROWS]
        peer_out[part, :, recv] = result[ROWS:]
    key_terms = dot(score_grad, queries) * SCALE
    value_terms = dot(weights_low, grads)
    for part, terms in enumerate((key_terms, value_terms)):
        exact_out[part, :, local] = terms[:256]
        first_out[part, :, local] = terms[256:384]
        second_out[part, :, local] = terms[384:512]
        third_out[part, :, local] = terms[512:].astype(BF16)


def attend(core, start, heads, q, g, k, v, qg_recv, kv_recv, first, second, third, chain, after):
    in_vmem = pl.BlockSpec(memory_space=pltpu.VMEM)
    width = heads * HEAD_DIM
    chain = list(chain) if chain is not None else []
    return pl.pallas_call(
        functools.partial(attend_kernel, start, heads),
        in_specs=[pl.BlockSpec(memory_space=pltpu.SMEM)]
        + [in_vmem] * (9 + len(chain))
        + [ANYWHERE] * len(after),
        out_specs=[in_vmem] * 6,
        out_shape=[
            jax.ShapeDtypeStruct((2, ROWS, HALF), BF16),
            jax.ShapeDtypeStruct((2, ROWS, HALF), BF16),
            jax.ShapeDtypeStruct((2, BLOCK, width), F32),
            jax.ShapeDtypeStruct((2, ROWS, width), F32),
            jax.ShapeDtypeStruct((2, ROWS, width), F32),
            jax.ShapeDtypeStruct((2, ROWS, width), BF16),
        ],
        input_output_aliases={10: 0, 11: 1} if chain else {},
        cost_estimate=COST,
        compiler_params=pltpu.CompilerParams(vmem_limit_bytes=VMEM_LIMIT),
        name="attend",
    )(core, q, g, k, v, qg_recv, kv_recv, first, second, third, *chain, *after)


def back_second_kernel(second_ref, third_ref, *refs):
    out_ref = refs[-1]
    pairs = spreader(64, 2)
    for part in range(2):
        out_ref[part] = (second_ref[part] + dot(pairs, third_ref[part, 64:])).astype(BF16)


def back_first_kernel(first_ref, second_ref, third_ref, *refs):
    out_ref = refs[-1]
    pairs = spreader(64, 2)
    fours = spreader(32, 4)
    for part in range(2):
        out_ref[part] = (
            first_ref[part]
            + dot(pairs, second_ref[part, 64:])
            + dot(fours, third_ref[part, 32:64])
        ).astype(BF16)


def finish_kernel(start, heads, exact_ref, first_ref, second_ref, third_ref, *refs):
    own_out, peer_out, token, total_ref, sems = refs[-5:]
    token[...] = jnp.zeros_like(token)
    weights = jnp.concatenate(
        [spreader(128, 2), spreader(64, 4), spreader(32, 8)], axis=1
    )
    for part in range(2):
        rows = jnp.concatenate(
            [first_ref[part], second_ref[part, :64], third_ref[part, :32]], axis=0
        )
        total_ref[part] = (exact_ref[part] + dot(weights, rows)).astype(BF16)
    lanes = pl.ds(start * HEAD_DIM, heads * HEAD_DIM)
    copies = [
        pltpu.make_async_copy(
            total_ref.at[:, pl.ds(part * ROWS, ROWS)], out.at[:, :, lanes], sems.at[part]
        )
        for part, out in enumerate((own_out, peer_out))
    ]
    for copy in copies:
        copy.start()
    for copy in copies:
        copy.wait()


def finish(start, heads, exact, first, second, third, chain, after):
    in_vmem = pl.BlockSpec(memory_space=pltpu.VMEM)
    chain = list(chain) if chain is not None else []
    return pl.pallas_call(
        functools.partial(finish_kernel, start, heads),
        in_specs=[in_vmem] * 4 + [ANYWHERE] * (len(chain) + len(after)),
        out_specs=[ANYWHERE, ANYWHERE, in_vmem],
        out_shape=[jax.ShapeDtypeStruct((2, ROWS, HALF), BF16)] * 2
        + [jax.ShapeDtypeStruct((8, 128), F32)],
        scratch_shapes=[
            pltpu.VMEM((2, BLOCK, heads * HEAD_DIM), BF16),
            pltpu.SemaphoreType.DMA((2,)),
        ],
        input_output_aliases={4: 0, 5: 1} if chain else {},
        cost_estimate=COST,
        compiler_params=pltpu.CompilerParams(vmem_limit_bytes=VMEM_LIMIT),
        name="finish",
    )(exact, first, second, third, *chain, *after)


def assemble_kernel(core, own_ref, recv_ref, *refs):
    a_ref, b_ref, token = refs[-3:]
    token[...] = jnp.zeros_like(token)
    mine = pl.program_id(0) == core[0]

    @pl.when(mine)
    def _():
        a_ref[...] = own_ref[0]
        b_ref[...] = own_ref[1]

    @pl.when(jnp.logical_not(mine))
    def _():
        a_ref[...] = recv_ref[0]
        b_ref[...] = recv_ref[1]


def assemble(core, own, recv, after):
    whole = pl.BlockSpec((2, ROWS, HALF), lambda j, c: (0, 0, 0))
    half = pl.BlockSpec((ROWS, HALF), lambda j, c: (0, j))
    return pl.pallas_call(
        assemble_kernel,
        grid_spec=pltpu.PrefetchScalarGridSpec(
            num_scalar_prefetch=1, grid=(2,), in_specs=[whole, whole] + [ANYWHERE] * len(after),
            out_specs=[half, half, pl.BlockSpec((8, 128), lambda j, c: (0, 0))],
        ),
        out_shape=[jax.ShapeDtypeStruct((ROWS, 2 * HALF), BF16)] * 2
        + [jax.ShapeDtypeStruct((8, 128), F32)],
        cost_estimate=COST,
        compiler_params=params(),
        name="assemble",
    )(core, own, recv, *after)


def swap_core(block):
    return lax.ppermute(block, "fine", [(i, i ^ 1) for i in range(lax.axis_size("fine"))])


def swap_fine(block, mask):
    return lax.ppermute(block, "fine", [(i, i ^ mask) for i in range(lax.axis_size("fine"))])


def swap_next(block, odd):
    fine, coarse = lax.axis_size("fine"), lax.axis_size("coarse")
    route = []
    for f in range(fine):
        for c in range(coarse):
            z = (f // 2) * 2 + c % 2
            if odd:
                there = (z + 1 if z % 2 else z - 1) % fine
            else:
                there = z ^ 1
            route.append((f * coarse + c, (there // 2 * 2 + f % 2) * coarse + c - c % 2 + there % 2))
    return lax.ppermute(block, ("fine", "coarse"), route)


def body(query_rows, key_rows, value_rows, out_grad):
    full_shape = query_rows.shape
    queries, keys, values, grads = (
        block.reshape(ROWS, 2 * HALF) for block in (query_rows, key_rows, value_rows, out_grad)
    )
    core = (lax.axis_index("fine") % 2).astype(jnp.int32).reshape(1)
    count = len(CHUNKS)
    starts = [sum(CHUNKS[:n]) for n in range(count)]
    own_packed, first, second, third = ([None] * count for _ in range(4))
    results, third_back, second_back, first_back = ([None] * count for _ in range(4))
    a_chain, b_chain, a_recv, after = None, None, None, []

    def shape_of(n):
        return jax.ShapeDtypeStruct((2, ROWS, CHUNKS[n] * HEAD_DIM), BF16)

    for step in ORDER:
        kind, n = step[0], int(step[1:])
        if kind == "K":
            send = extract_other(core, keys, values, after, VMEM_LIMIT)
            kv_recv = swap_core(send)
        elif kind == "Q":
            send = extract_other(core, queries, grads, after, VMEM_LIMIT)
            qg_recv = swap_core(send)
        elif kind == "A":
            packed = pack_first(core, keys, values, kv_recv, after)
            own_packed = packed[1::2]
            first = [swap_fine(rows, 2) for rows in packed[::2]]
            send = packed[0]
        elif kind == "B":
            send = whole_call(
                pack_second_kernel, "pack_second", shape_of(n), after, own_packed[n], first[n]
            )
            second[n] = swap_fine(send, 6)
        elif kind == "D":
            send = whole_call(
                pack_third_kernel, "pack_third", shape_of(n), after, own_packed[n], first[n], second[n]
            )
            third[n] = swap_next(send, PARITY[n])
        elif kind == "E":
            results[n] = attend(
                core, starts[n], CHUNKS[n], queries, grads, keys, values, qg_recv, kv_recv,
                first[n], second[n], third[n], a_chain, after,
            )
            a_chain = results[n][:2]
            send = results[n][5]
            third_back[n] = swap_next(send, PARITY[n])
        elif kind == "F":
            send = whole_call(
                back_second_kernel, "back_second", shape_of(n), after, results[n][4], third_back[n]
            )
            second_back[n] = swap_fine(send, 6)
        elif kind == "G":
            send = whole_call(
                back_first_kernel, "back_first", shape_of(n), after,
                results[n][3], second_back[n], third_back[n],
            )
            first_back[n] = swap_fine(send, 2)
        elif kind == "H":
            *b_chain, send = finish(
                starts[n], CHUNKS[n], results[n][2], first_back[n], second_back[n], third_back[n],
                b_chain, after,
            )
        elif kind == "S":
            a_recv = swap_core(a_chain[1])
            continue
        elif kind == "R":
            after = after + [qg_recv]
            continue
        elif kind == "T":
            attended, query_grad, send = assemble(core, a_chain[0], a_recv, after)
        after = [send]
    b_recv = swap_core(b_chain[1])
    key_grad, value_grad, _ = assemble(core, b_chain[0], b_recv, after)
    return tuple(
        block.reshape(full_shape) for block in (attended, query_grad, key_grad, value_grad)
    )


def solution(mesh):
    placed = P("coarse", "fine", None, None)
    return jax.shard_map(
        body, mesh=mesh, in_specs=(placed,) * 4, out_specs=(placed,) * 4, check_vma=False
    )
```

profile of v0, /device:TPU:1, one launch (start us, length us, event | category | flops | bytes accessed | tf_op | source)
XLA Modules:
  0.0 132.5 jit_solution(12951487806277243974)
XLA Ops:
  0.7 1.1 copy-done
  1.8 1.1 copy-done.2
  3.0 3.3 %collective-permute-start.1 = (bf16[2,128,1536]{2,1,0:T(8,128)(2,1)S(1)}, bf16[2,128,1536]{2,1,0:T(8,128)(2,1)S(1)}, u32[]{:S(2)}, u32[]{:S(2)}) collective-permute-start(bf16[2,128,1536]{2,1,0:T(8,128)(2,1)S(1)} %extract_other.2.refs_0_), channel_id=1, source_target_pairs={{0,32},{32,0},{64,96},{96,64},{128,160},{160,128},{192,224},{224,1... | collective-permute-start | bytes 2359304 | tf_op jit(solution)/shard_map/ppermute | solution.py:326
  6.4 1.3 collective-permute-start
  7.7 0.5 collective-permute-done.1.kv_ref.refs_1_
  8.2 0.6 pack_first.1
  8.9 1.3 %collective-permute-start.4 = (bf16[2,128,384]{2,1,0:T(8,128)(2,1)S(1)}, bf16[2,128,384]{2,1,0:T(8,128)(2,1)S(1)}, u32[]{:S(2)}, u32[]{:S(2)}) collective-permute-start(bf16[2,128,384]{2,1,0:T(8,128)(2,1)S(1)} %get-tuple-element.58), channel_id=1, source_target_pairs={{0,64},{32,96},{64,0},{96,32},{128,192},{160,224},{192,128},{224,1... | collective-permute-start | bytes 589832 | tf_op jit(solution)/shard_map/ppermute | solution.py:330
  10.2 1.1 collective-permute-start.6
  11.3 13.5 %collective-permute-done.4.first_ref.refs_2_ = bf16[2,128,384]{2,1,0:T(8,128)(2,1)S(1)} collective-permute-done((bf16[2,128,384]{2,1,0:T(8,128)(2,1)S(1)}, bf16[2,128,384]{2,1,0:T(8,128)(2,1)S(1)}, u32[]{:S(2)}, u32[]{:S(2)}) %collective-permute-start.4) | collective-permute-done | bytes 196640 | tf_op jit(solution)/shard_map/ppermute | solution.py:330
  25.0 2.3 %collective-permute-start.5 = (bf16[2,128,384]{2,1,0:T(8,128)(2,1)S(1)}, bf16[2,128,384]{2,1,0:T(8,128)(2,1)S(1)}, u32[]{:S(2)}, u32[]{:S(2)}) collective-permute-start(bf16[2,128,384]{2,1,0:T(8,128)(2,1)S(1)} %pack_second.4.refs_0_), channel_id=1, source_target_pairs={{0,192},{32,224},{64,128},{96,160},{128,64},{160,96},{192,0},{224,... | collective-permute-start | bytes 589832 | tf_op jit(solution)/shard_map/ppermute | solution.py:330
  27.3 3.1 %collective-permute-start.3 = (bf16[2,128,384]{2,1,0:T(8,128)(2,1)S(1)}, bf16[2,128,384]{2,1,0:T(8,128)(2,1)S(1)}, u32[]{:S(2)}, u32[]{:S(2)}) collective-permute-start(bf16[2,128,384]{2,1,0:T(8,128)(2,1)S(1)} %get-tuple-element.56), channel_id=1, source_target_pairs={{0,64},{32,96},{64,0},{96,32},{128,192},{160,224},{192,128},{224,1... | collective-permute-start | bytes 589832 | tf_op jit(solution)/shard_map/ppermute | solution.py:330
  30.6 0.9 collective-permute-start.8
  31.5 13.1 %collective-permute-done.5.second_ref.refs_3_ = bf16[2,128,384]{2,1,0:T(8,128)(2,1)S(1)} collective-permute-done((bf16[2,128,384]{2,1,0:T(8,128)(2,1)S(1)}, bf16[2,128,384]{2,1,0:T(8,128)(2,1)S(1)}, u32[]{:S(2)}, u32[]{:S(2)}) %collective-permute-start.5) | collective-permute-done | bytes 196640 | tf_op jit(solution)/shard_map/ppermute | solution.py:330
  45.0 0.6 collective-permute-start.11
  45.9 3.1 %collective-permute-done.8.second_ref.refs_3_ = bf16[2,128,384]{2,1,0:T(8,128)(2,1)S(1)} collective-permute-done((bf16[2,128,384]{2,1,0:T(8,128)(2,1)S(1)}, bf16[2,128,384]{2,1,0:T(8,128)(2,1)S(1)}, u32[]{:S(2)}, u32[]{:S(2)}) %collective-permute-start.8) | collective-permute-done | bytes 196640 | tf_op jit(solution)/shard_map/ppermute | solution.py:330
  49.2 1.9 %collective-permute-start.7 = (bf16[2,128,384]{2,1,0:T(8,128)(2,1)S(1)}, bf16[2,128,384]{2,1,0:T(8,128)(2,1)S(1)}, u32[]{:S(2)}, u32[]{:S(2)}) collective-permute-start(bf16[2,128,384]{2,1,0:T(8,128)(2,1)S(1)} %pack_second.7.refs_0_), channel_id=1, source_target_pairs={{0,192},{32,224},{64,128},{96,160},{128,64},{160,96},{192,0},{224,... | collective-permute-start | bytes 589832 | tf_op jit(solution)/shard_map/ppermute | solution.py:330
  51.1 2.5 %collective-permute-done.10.refs_4_ = bf16[2,128,384]{2,1,0:T(8,128)(2,1)S(1)} collective-permute-done((bf16[2,128,384]{2,1,0:T(8,128)(2,1)S(1)}, bf16[2,128,384]{2,1,0:T(8,128)(2,1)S(1)}, u32[]{:S(2)}, u32[]{:S(2)}) %collective-permute-start.10) | collective-permute-done | bytes 196640 | tf_op jit(solution)/shard_map/ppermute | solution.py:344
  53.6 2.8 %attend.4 = (bf16[2,128,1536]{2,1,0:T(8,128)(2,1)S(1)}, bf16[2,128,1536]{2,1,0:T(8,128)(2,1)S(1)}, f32[2,256,384]{2,1,0:T(8,128)S(1)}, f32[2,128,384]{2,1,0:T(8,...) custom-call(s32[1]{0:T(128)} %bitcast.core, bf16[128,3072]{1,0:T(8,128)(2,1)S(1)} %bitcast.22, ...), custom_call_target="tpu_custom_call" | custom-call | flops 1 | bytes 1 | tf_op jit(solution)/shard_map/attend/pallas_call | solution.py:208
  56.4 2.4 %collective-permute-start.14 = (bf16[2,128,384]{2,1,0:T(8,128)(2,1)S(1)}, bf16[2,128,384]{2,1,0:T(8,128)(2,1)S(1)}, u32[]{:S(2)}, u32[]{:S(2)}) collective-permute-start(bf16[2,128,384]{2,1,0:T(8,128)(2,1)S(1)} %get-tuple-element.63.refs_0_), channel_id=1, source_target_pairs={{0,1},{1,0},{2,3},{3,2},{4,5},{5,4},{6,7},{7,6},{8,9},{9,8},{10,11... | collective-permute-start | bytes 589832 | tf_op jit(solution)/shard_map/ppermute | solution.py:344
  59.0 2.1 %collective-permute-start.13 = (bf16[2,128,384]{2,1,0:T(8,128)(2,1)S(1)}, bf16[2,128,384]{2,1,0:T(8,128)(2,1)S(1)}, u32[]{:S(2)}, u32[]{:S(2)}) collective-permute-start(bf16[2,128,384]{2,1,0:T(8,128)(2,1)S(1)} %pack_third.6.refs_7_), channel_id=1, source_target_pairs={{0,193},{1,64},{2,195},{3,66},{4,197},{5,68},{6,199},{7,70},{8,201... | collective-permute-start | bytes 589832 | tf_op jit(solution)/shard_map/ppermute | solution.py:344
  61.1 0.9 collective-permute-done.9.refs_4_
  62.1 2.8 %attend.5 = (bf16[2,128,1536]{2,1,0:T(8,128)(2,1)S(1)}, bf16[2,128,1536]{2,1,0:T(8,128)(2,1)S(1)}, f32[2,256,384]{2,1,0:T(8,128)S(1)}, f32[2,128,384]{2,1,0:T(8,...) custom-call(s32[1]{0:T(128)} %bitcast.core, ...), custom_call_target="tpu_custom_call", output_to_operand_aliasing={{0}: (10, {}), {1}: (11, {})} | custom-call | flops 1 | bytes 1 | tf_op jit(solution)/shard_map/attend/pallas_call | solution.py:208
  64.8 1.8 %collective-permute-done.7.second_ref.refs_3_ = bf16[2,128,384]{2,1,0:T(8,128)(2,1)S(1)} collective-permute-done((bf16[2,128,384]{2,1,0:T(8,128)(2,1)S(1)}, bf16[2,128,384]{2,1,0:T(8,128)(2,1)S(1)}, u32[]{:S(2)}, u32[]{:S(2)}) %collective-permute-start.7) | collective-permute-done | bytes 196640 | tf_op jit(solution)/shard_map/ppermute | solution.py:330
  66.9 1.5 %collective-permute-start.12 = (bf16[2,128,384]{2,1,0:T(8,128)(2,1)S(1)}, bf16[2,128,384]{2,1,0:T(8,128)(2,1)S(1)}, u32[]{:S(2)}, u32[]{:S(2)}) collective-permute-start(bf16[2,128,384]{2,1,0:T(8,128)(2,1)S(1)} %pack_third.7.refs_0_), channel_id=1, source_target_pairs={{0,1},{1,0},{2,3},{3,2},{4,5},{5,4},{6,7},{7,6},{8,9},{9,8},{10,11... | collective-permute-start | bytes 589832 | tf_op jit(solution)/shard_map/ppermute | solution.py:344
  68.6 1.8 %collective-permute-start.19 = (bf16[2,128,384]{2,1,0:T(8,128)(2,1)S(1)}, bf16[2,128,384]{2,1,0:T(8,128)(2,1)S(1)}, u32[]{:S(2)}, u32[]{:S(2)}) collective-permute-start(bf16[2,128,384]{2,1,0:T(8,128)(2,1)S(1)} %back_second.4.refs_7_), channel_id=1, source_target_pairs={{0,192},{32,224},{64,128},{96,160},{128,64},{160,96},{192,0},{224,... | collective-permute-start | bytes 589832 | tf_op jit(solution)/shard_map/ppermute | solution.py:330
  70.4 0.7 collective-permute-done.13.refs_4_
  71.1 2.7 %attend.6 = (bf16[2,128,1536]{2,1,0:T(8,128)(2,1)S(1)}, bf16[2,128,1536]{2,1,0:T(8,128)(2,1)S(1)}, f32[2,256,384]{2,1,0:T(8,128)S(1)}, f32[2,128,384]{2,1,0:T(8,...) custom-call(s32[1]{0:T(128)} %bitcast.core, ...), custom_call_target="tpu_custom_call", output_to_operand_aliasing={{0}: (10, {}), {1}: (11, {})} | custom-call | flops 1 | bytes 1 | tf_op jit(solution)/shard_map/attend/pallas_call | solution.py:208
  73.8 0.6 collective-permute-start.18
  74.4 1.8 %collective-permute-start.17 = (bf16[2,128,384]{2,1,0:T(8,128)(2,1)S(1)}, bf16[2,128,384]{2,1,0:T(8,128)(2,1)S(1)}, u32[]{:S(2)}, u32[]{:S(2)}) collective-permute-start(bf16[2,128,384]{2,1,0:T(8,128)(2,1)S(1)} %get-tuple-element.64.refs_0_), channel_id=1, source_target_pairs={{0,1},{1,0},{2,3},{3,2},{4,5},{5,4},{6,7},{7,6},{8,9},{9,8},{10,11... | collective-permute-start | bytes 589832 | tf_op jit(solution)/shard_map/ppermute | solution.py:344
  76.2 2.7 %attend.7 = (bf16[2,128,1536]{2,1,0:T(8,128)(2,1)S(1)}, bf16[2,128,1536]{2,1,0:T(8,128)(2,1)S(1)}, f32[2,256,384]{2,1,0:T(8,128)S(1)}, f32[2,128,384]{2,1,0:T(8,...) custom-call(s32[1]{0:T(128)} %bitcast.core, ...), custom_call_target="tpu_custom_call", output_to_operand_aliasing={{0}: (10, {}), {1}: (11, {})} | custom-call | flops 1 | bytes 1 | tf_op jit(solution)/shard_map/attend/pallas_call | solution.py:208
  79.0 1.5 %collective-permute-start.15 = (bf16[2,128,1536]{2,1,0:T(8,128)(2,1)S(1)}, bf16[2,128,1536]{2,1,0:T(8,128)(2,1)S(1)}, u32[]{:S(2)}, u32[]{:S(2)}) collective-permute-start(bf16[2,128,1536]{2,1,0:T(8,128)(2,1)S(1)} %get-tuple-element.72), channel_id=1, source_target_pairs={{0,32},{32,0},{64,96},{96,64},{128,160},{160,128},{192,224},{224,1... | collective-permute-start | bytes 2359304 | tf_op jit(solution)/shard_map/ppermute | solution.py:326
  80.5 0.5 collective-permute-start.16
  81.2 3.1 %collective-permute-done.18.third_ref = bf16[2,128,384]{2,1,0:T(8,128)(2,1)S(1)} collective-permute-done((bf16[2,128,384]{2,1,0:T(8,128)(2,1)S(1)}, bf16[2,128,384]{2,1,0:T(8,128)(2,1)S(1)}, u32[]{:S(2)}, u32[]{:S(2)}) %collective-permute-start.18) | collective-permute-done | bytes 196640 | tf_op jit(solution)/shard_map/ppermute | solution.py:344
  85.0 3.3 %collective-permute-start.21 = (bf16[2,128,384]{2,1,0:T(8,128)(2,1)S(1)}, bf16[2,128,384]{2,1,0:T(8,128)(2,1)S(1)}, u32[]{:S(2)}, u32[]{:S(2)}) collective-permute-start(bf16[2,128,384]{2,1,0:T(8,128)(2,1)S(1)} %back_first.4.refs_0_), channel_id=1, source_target_pairs={{0,64},{32,96},{64,0},{96,32},{128,192},{160,224},{192,128},{224,1... | collective-permute-start | bytes 589832 | tf_op jit(solution)/shard_map/ppermute | solution.py:330
  88.5 0.7 collective-permute-start.20
  89.2 8.8 %collective-permute-done.22.second_ref = bf16[2,128,384]{2,1,0:T(8,128)(2,1)S(1)} collective-permute-done((bf16[2,128,384]{2,1,0:T(8,128)(2,1)S(1)}, bf16[2,128,384]{2,1,0:T(8,128)(2,1)S(1)}, u32[]{:S(2)}, u32[]{:S(2)}) %collective-permute-start.22) | collective-permute-done | bytes 196640 | tf_op jit(solution)/shard_map/ppermute | solution.py:330
  98.3 3.0 %collective-permute-start.25 = (bf16[2,128,384]{2,1,0:T(8,128)(2,1)S(1)}, bf16[2,128,384]{2,1,0:T(8,128)(2,1)S(1)}, u32[]{:S(2)}, u32[]{:S(2)}) collective-permute-start(bf16[2,128,384]{2,1,0:T(8,128)(2,1)S(1)} %back_second.5.refs_0_), channel_id=1, source_target_pairs={{0,192},{32,224},{64,128},{96,160},{128,64},{160,96},{192,0},{224,... | collective-permute-start | bytes 589832 | tf_op jit(solution)/shard_map/ppermute | solution.py:330
  101.3 0.4 finish.4
  101.7 0.5 collective-permute-done.20.second_ref
  102.4 5.3 %collective-permute-start.23 = (bf16[2,128,384]{2,1,0:T(8,128)(2,1)S(1)}, bf16[2,128,384]{2,1,0:T(8,128)(2,1)S(1)}, u32[]{:S(2)}, u32[]{:S(2)}) collective-permute-start(bf16[2,128,384]{2,1,0:T(8,128)(2,1)S(1)} %back_first.6.refs_2_), channel_id=1, source_target_pairs={{0,64},{32,96},{64,0},{96,32},{128,192},{160,224},{192,128},{224,1... | collective-permute-start | bytes 589832 | tf_op jit(solution)/shard_map/ppermute | solution.py:330
  108.5 3.5 %collective-permute-start.26 = (bf16[2,128,384]{2,1,0:T(8,128)(2,1)S(1)}, bf16[2,128,384]{2,1,0:T(8,128)(2,1)S(1)}, u32[]{:S(2)}, u32[]{:S(2)}) collective-permute-start(bf16[2,128,384]{2,1,0:T(8,128)(2,1)S(1)} %back_first.7.refs_2_), channel_id=1, source_target_pairs={{0,64},{32,96},{64,0},{96,32},{128,192},{160,224},{192,128},{224,1... | collective-permute-start | bytes 589832 | tf_op jit(solution)/shard_map/ppermute | solution.py:330
  112.0 4.0 %collective-permute-done.23.first_ref = bf16[2,128,384]{2,1,0:T(8,128)(2,1)S(1)} collective-permute-done((bf16[2,128,384]{2,1,0:T(8,128)(2,1)S(1)}, bf16[2,128,384]{2,1,0:T(8,128)(2,1)S(1)}, u32[]{:S(2)}, u32[]{:S(2)}) %collective-permute-start.23) | collective-permute-done | bytes 196640 | tf_op jit(solution)/shard_map/ppermute | solution.py:330
  116.0 0.4 finish.6
  116.4 1.2 assemble.2
  117.6 9.5 %collective-permute-done.26.first_ref = bf16[2,128,384]{2,1,0:T(8,128)(2,1)S(1)} collective-permute-done((bf16[2,128,384]{2,1,0:T(8,128)(2,1)S(1)}, bf16[2,128,384]{2,1,0:T(8,128)(2,1)S(1)}, u32[]{:S(2)}, u32[]{:S(2)}) %collective-permute-start.26) | collective-permute-done | bytes 196640 | tf_op jit(solution)/shard_map/ppermute | solution.py:330
  127.6 1.8 %collective-permute-start.27 = (bf16[2,128,1536]{2,1,0:T(8,128)(2,1)S(1)}, bf16[2,128,1536]{2,1,0:T(8,128)(2,1)S(1)}, u32[]{:S(2)}, u32[]{:S(2)}) collective-permute-start(bf16[2,128,1536]{2,1,0:T(8,128)(2,1)S(1)} %get-tuple-element.98), channel_id=1, source_target_pairs={{0,32},{32,0},{64,96},{96,64},{128,160},{160,128},{192,224},{224,1... | collective-permute-start | bytes 2359304 | tf_op jit(solution)/shard_map/ppermute | solution.py:326
  129.4 1.9 %collective-permute-done.27.recv_ref = bf16[2,128,1536]{2,1,0:T(8,128)(2,1)S(1)} collective-permute-done((bf16[2,128,1536]{2,1,0:T(8,128)(2,1)S(1)}, bf16[2,128,1536]{2,1,0:T(8,128)(2,1)S(1)}, u32[]{:S(2)}, u32[]{:S(2)}) %collective-permute-start.27) | collective-permute-done | bytes 786464 | tf_op jit(solution)/shard_map/ppermute | solution.py:326
  131.3 1.2 assemble.3
  (49 shorter events, 4.9 us)
Async XLA Ops:
  0.6 1.1 copy-start
  1.8 1.1 copy-start.2
  2.9 3.4 %copy-start.4 = (bf16[1,1,128,3072]{3,2,1,0:T(8,128)(2,1)S(1)}, bf16[1,1,128,3072]{3,2,1,0:T(8,128)(2,1)}, u32[]{:S(2)}) copy-start(bf16[1,1,128,3072]{3,2,1,0:T(8,128)(2,1)} %param.4) | copy-start | bytes 2359300
  2.9 3.4 %copy-start.5 = (bf16[1,1,128,3072]{3,2,1,0:T(8,128)(2,1)S(1)}, bf16[1,1,128,3072]{3,2,1,0:T(8,128)(2,1)}, u32[]{:S(2)}) copy-start(bf16[1,1,128,3072]{3,2,1,0:T(8,128)(2,1)} %param.7) | copy-start | bytes 2359300
  3.0 5.2 %collective-permute-start.1 = (bf16[2,128,1536]{2,1,0:T(8,128)(2,1)S(1)}, bf16[2,128,1536]{2,1,0:T(8,128)(2,1)S(1)}, u32[]{:S(2)}, u32[]{:S(2)}) collective-permute-start(bf16[2,128,1536]{2,1,0:T(8,128)(2,1)S(1)} %extract_other.2.refs_0_), channel_id=1, source_target_pairs={{0,32},{32,0},{64,96},{96,64},{128,160},{160,128},{192,224},{224,1... | collective-permute-start | bytes 2359304 | tf_op jit(solution)/shard_map/ppermute | solution.py:326
  6.3 1.9 %copy-start.1 = (bf16[1,1,128,3072]{3,2,1,0:T(8,128)(2,1)S(1)}, bf16[1,1,128,3072]{3,2,1,0:T(8,128)(2,1)}, u32[]{:S(2)}) copy-start(bf16[1,1,128,3072]{3,2,1,0:T(8,128)(2,1)} %param.5) | copy-start | bytes 2359300
  6.3 1.9 %copy-start.3 = (bf16[1,1,128,3072]{3,2,1,0:T(8,128)(2,1)S(1)}, bf16[1,1,128,3072]{3,2,1,0:T(8,128)(2,1)}, u32[]{:S(2)}) copy-start(bf16[1,1,128,3072]{3,2,1,0:T(8,128)(2,1)} %param.6) | copy-start | bytes 2359300
  6.4 44.7 %collective-permute-start = (bf16[2,128,1536]{2,1,0:T(8,128)(2,1)S(1)}, bf16[2,128,1536]{2,1,0:T(8,128)(2,1)S(1)}, u32[]{:S(2)}, u32[]{:S(2)}) collective-permute-start(bf16[2,128,1536]{2,1,0:T(8,128)(2,1)S(1)} %extract_other.3.refs_0_), channel_id=1, source_target_pairs={{0,32},{32,0},{64,96},{96,64},{128,160},{160,128},{192,224},{224,1... | collective-permute-start | bytes 2359304 | tf_op jit(solution)/shard_map/ppermute | solution.py:326
  8.9 16.0 %collective-permute-start.4 = (bf16[2,128,384]{2,1,0:T(8,128)(2,1)S(1)}, bf16[2,128,384]{2,1,0:T(8,128)(2,1)S(1)}, u32[]{:S(2)}, u32[]{:S(2)}) collective-permute-start(bf16[2,128,384]{2,1,0:T(8,128)(2,1)S(1)} %get-tuple-element.58), channel_id=1, source_target_pairs={{0,64},{32,96},{64,0},{96,32},{128,192},{160,224},{192,128},{224,1... | collective-permute-start | bytes 589832 | tf_op jit(solution)/shard_map/ppermute | solution.py:330
  10.2 20.2 %collective-permute-start.6 = (bf16[2,128,384]{2,1,0:T(8,128)(2,1)S(1)}, bf16[2,128,384]{2,1,0:T(8,128)(2,1)S(1)}, u32[]{:S(2)}, u32[]{:S(2)}) collective-permute-start(bf16[2,128,384]{2,1,0:T(8,128)(2,1)S(1)} %get-tuple-element.60), channel_id=1, source_target_pairs={{0,64},{32,96},{64,0},{96,32},{128,192},{160,224},{192,128},{224,1... | collective-permute-start | bytes 589832 | tf_op jit(solution)/shard_map/ppermute | solution.py:330
  25.0 19.5 %collective-permute-start.5 = (bf16[2,128,384]{2,1,0:T(8,128)(2,1)S(1)}, bf16[2,128,384]{2,1,0:T(8,128)(2,1)S(1)}, u32[]{:S(2)}, u32[]{:S(2)}) collective-permute-start(bf16[2,128,384]{2,1,0:T(8,128)(2,1)S(1)} %pack_second.4.refs_0_), channel_id=1, source_target_pairs={{0,192},{32,224},{64,128},{96,160},{128,64},{160,96},{192,0},{224,... | collective-permute-start | bytes 589832 | tf_op jit(solution)/shard_map/ppermute | solution.py:330
  27.3 17.6 %collective-permute-start.3 = (bf16[2,128,384]{2,1,0:T(8,128)(2,1)S(1)}, bf16[2,128,384]{2,1,0:T(8,128)(2,1)S(1)}, u32[]{:S(2)}, u32[]{:S(2)}) collective-permute-start(bf16[2,128,384]{2,1,0:T(8,128)(2,1)S(1)} %get-tuple-element.56), channel_id=1, source_target_pairs={{0,64},{32,96},{64,0},{96,32},{128,192},{160,224},{192,128},{224,1... | collective-permute-start | bytes 589832 | tf_op jit(solution)/shard_map/ppermute | solution.py:330
  30.4 15.3 %collective-permute-start.2 = (bf16[2,128,384]{2,1,0:T(8,128)(2,1)S(1)}, bf16[2,128,384]{2,1,0:T(8,128)(2,1)S(1)}, u32[]{:S(2)}, u32[]{:S(2)}) collective-permute-start(bf16[2,128,384]{2,1,0:T(8,128)(2,1)S(1)} %get-tuple-element.53.refs_0_), channel_id=1, source_target_pairs={{0,64},{32,96},{64,0},{96,32},{128,192},{160,224},{192,128},{224,1... | collective-permute-start | bytes 589832 | tf_op jit(solution)/shard_map/ppermute | solution.py:330
  30.6 18.4 %collective-permute-start.8 = (bf16[2,128,384]{2,1,0:T(8,128)(2,1)S(1)}, bf16[2,128,384]{2,1,0:T(8,128)(2,1)S(1)}, u32[]{:S(2)}, u32[]{:S(2)}) collective-permute-start(bf16[2,128,384]{2,1,0:T(8,128)(2,1)S(1)} %pack_second.5.refs_0_), channel_id=1, source_target_pairs={{0,192},{32,224},{64,128},{96,160},{128,64},{160,96},{192,0},{224,... | collective-permute-start | bytes 589832 | tf_op jit(solution)/shard_map/ppermute | solution.py:330
  44.7 8.9 %collective-permute-start.10 = (bf16[2,128,384]{2,1,0:T(8,128)(2,1)S(1)}, bf16[2,128,384]{2,1,0:T(8,128)(2,1)S(1)}, u32[]{:S(2)}, u32[]{:S(2)}) collective-permute-start(bf16[2,128,384]{2,1,0:T(8,128)(2,1)S(1)} %pack_third.4.refs_0_), channel_id=1, source_target_pairs={{0,1},{1,0},{2,3},{3,2},{4,5},{5,4},{6,7},{7,6},{8,9},{9,8},{10,11... | collective-permute-start | bytes 589832 | tf_op jit(solution)/shard_map/ppermute | solution.py:344
  45.0 13.8 %collective-permute-start.11 = (bf16[2,128,384]{2,1,0:T(8,128)(2,1)S(1)}, bf16[2,128,384]{2,1,0:T(8,128)(2,1)S(1)}, u32[]{:S(2)}, u32[]{:S(2)}) collective-permute-start(bf16[2,128,384]{2,1,0:T(8,128)(2,1)S(1)} %pack_second.6.refs_0_), channel_id=1, source_target_pairs={{0,192},{32,224},{64,128},{96,160},{128,64},{160,96},{192,0},{224,... | collective-permute-start | bytes 589832 | tf_op jit(solution)/shard_map/ppermute | solution.py:330
  49.1 12.9 %collective-permute-start.9 = (bf16[2,128,384]{2,1,0:T(8,128)(2,1)S(1)}, bf16[2,128,384]{2,1,0:T(8,128)(2,1)S(1)}, u32[]{:S(2)}, u32[]{:S(2)}) collective-permute-start(bf16[2,128,384]{2,1,0:T(8,128)(2,1)S(1)} %pack_third.5.refs_5_), channel_id=1, source_target_pairs={{0,1},{1,0},{2,3},{3,2},{4,5},{5,4},{6,7},{7,6},{8,9},{9,8},{10,11... | collective-permute-start | bytes 589832 | tf_op jit(solution)/shard_map/ppermute | solution.py:344
  49.2 17.4 %collective-permute-start.7 = (bf16[2,128,384]{2,1,0:T(8,128)(2,1)S(1)}, bf16[2,128,384]{2,1,0:T(8,128)(2,1)S(1)}, u32[]{:S(2)}, u32[]{:S(2)}) collective-permute-start(bf16[2,128,384]{2,1,0:T(8,128)(2,1)S(1)} %pack_second.7.refs_0_), channel_id=1, source_target_pairs={{0,192},{32,224},{64,128},{96,160},{128,64},{160,96},{192,0},{224,... | collective-permute-start | bytes 589832 | tf_op jit(solution)/shard_map/ppermute | solution.py:330
  56.4 12.1 %collective-permute-start.14 = (bf16[2,128,384]{2,1,0:T(8,128)(2,1)S(1)}, bf16[2,128,384]{2,1,0:T(8,128)(2,1)S(1)}, u32[]{:S(2)}, u32[]{:S(2)}) collective-permute-start(bf16[2,128,384]{2,1,0:T(8,128)(2,1)S(1)} %get-tuple-element.63.refs_0_), channel_id=1, source_target_pairs={{0,1},{1,0},{2,3},{3,2},{4,5},{5,4},{6,7},{7,6},{8,9},{9,8},{10,11... | collective-permute-start | bytes 589832 | tf_op jit(solution)/shard_map/ppermute | solution.py:344
  59.0 12.1 %collective-permute-start.13 = (bf16[2,128,384]{2,1,0:T(8,128)(2,1)S(1)}, bf16[2,128,384]{2,1,0:T(8,128)(2,1)S(1)}, u32[]{:S(2)}, u32[]{:S(2)}) collective-permute-start(bf16[2,128,384]{2,1,0:T(8,128)(2,1)S(1)} %pack_third.6.refs_7_), channel_id=1, source_target_pairs={{0,193},{1,64},{2,195},{3,66},{4,197},{5,68},{6,199},{7,70},{8,201... | collective-permute-start | bytes 589832 | tf_op jit(solution)/shard_map/ppermute | solution.py:344
  66.9 9.4 %collective-permute-start.12 = (bf16[2,128,384]{2,1,0:T(8,128)(2,1)S(1)}, bf16[2,128,384]{2,1,0:T(8,128)(2,1)S(1)}, u32[]{:S(2)}, u32[]{:S(2)}) collective-permute-start(bf16[2,128,384]{2,1,0:T(8,128)(2,1)S(1)} %pack_third.7.refs_0_), channel_id=1, source_target_pairs={{0,1},{1,0},{2,3},{3,2},{4,5},{5,4},{6,7},{7,6},{8,9},{9,8},{10,11... | collective-permute-start | bytes 589832 | tf_op jit(solution)/shard_map/ppermute | solution.py:344
  68.6 12.3 %collective-permute-start.19 = (bf16[2,128,384]{2,1,0:T(8,128)(2,1)S(1)}, bf16[2,128,384]{2,1,0:T(8,128)(2,1)S(1)}, u32[]{:S(2)}, u32[]{:S(2)}) collective-permute-start(bf16[2,128,384]{2,1,0:T(8,128)(2,1)S(1)} %back_second.4.refs_7_), channel_id=1, source_target_pairs={{0,192},{32,224},{64,128},{96,160},{128,64},{160,96},{192,0},{224,... | collective-permute-start | bytes 589832 | tf_op jit(solution)/shard_map/ppermute | solution.py:330
  73.8 10.5 %collective-permute-start.18 = (bf16[2,128,384]{2,1,0:T(8,128)(2,1)S(1)}, bf16[2,128,384]{2,1,0:T(8,128)(2,1)S(1)}, u32[]{:S(2)}, u32[]{:S(2)}) collective-permute-start(bf16[2,128,384]{2,1,0:T(8,128)(2,1)S(1)} %get-tuple-element.70.refs_7_), channel_id=1, source_target_pairs={{0,193},{1,64},{2,195},{3,66},{4,197},{5,68},{6,199},{7,70},{8,201... | collective-permute-start | bytes 589832 | tf_op jit(solution)/shard_map/ppermute | solution.py:344
  74.4 10.1 %collective-permute-start.17 = (bf16[2,128,384]{2,1,0:T(8,128)(2,1)S(1)}, bf16[2,128,384]{2,1,0:T(8,128)(2,1)S(1)}, u32[]{:S(2)}, u32[]{:S(2)}) collective-permute-start(bf16[2,128,384]{2,1,0:T(8,128)(2,1)S(1)} %get-tuple-element.64.refs_0_), channel_id=1, source_target_pairs={{0,1},{1,0},{2,3},{3,2},{4,5},{5,4},{6,7},{7,6},{8,9},{9,8},{10,11... | collective-permute-start | bytes 589832 | tf_op jit(solution)/shard_map/ppermute | solution.py:344
  79.0 37.4 %collective-permute-start.15 = (bf16[2,128,1536]{2,1,0:T(8,128)(2,1)S(1)}, bf16[2,128,1536]{2,1,0:T(8,128)(2,1)S(1)}, u32[]{:S(2)}, u32[]{:S(2)}) collective-permute-start(bf16[2,128,1536]{2,1,0:T(8,128)(2,1)S(1)} %get-tuple-element.72), channel_id=1, source_target_pairs={{0,32},{32,0},{64,96},{96,64},{128,160},{160,128},{192,224},{224,1... | collective-permute-start | bytes 2359304 | tf_op jit(solution)/shard_map/ppermute | solution.py:326
  80.5 7.8 %collective-permute-start.16 = (bf16[2,128,384]{2,1,0:T(8,128)(2,1)S(1)}, bf16[2,128,384]{2,1,0:T(8,128)(2,1)S(1)}, u32[]{:S(2)}, u32[]{:S(2)}) collective-permute-start(bf16[2,128,384]{2,1,0:T(8,128)(2,1)S(1)} %get-tuple-element.76.refs_0_), channel_id=1, source_target_pairs={{0,1},{1,0},{2,3},{3,2},{4,5},{5,4},{6,7},{7,6},{8,9},{9,8},{10,11... | collective-permute-start | bytes 589832 | tf_op jit(solution)/shard_map/ppermute | solution.py:344
  84.7 13.3 %collective-permute-start.22 = (bf16[2,128,384]{2,1,0:T(8,128)(2,1)S(1)}, bf16[2,128,384]{2,1,0:T(8,128)(2,1)S(1)}, u32[]{:S(2)}, u32[]{:S(2)}) collective-permute-start(bf16[2,128,384]{2,1,0:T(8,128)(2,1)S(1)} %back_second.6.refs_0_), channel_id=1, source_target_pairs={{0,192},{32,224},{64,128},{96,160},{128,64},{160,96},{192,0},{224,... | collective-permute-start | bytes 589832 | tf_op jit(solution)/shard_map/ppermute | solution.py:330
  85.0 16.3 %collective-permute-start.21 = (bf16[2,128,384]{2,1,0:T(8,128)(2,1)S(1)}, bf16[2,128,384]{2,1,0:T(8,128)(2,1)S(1)}, u32[]{:S(2)}, u32[]{:S(2)}) collective-permute-start(bf16[2,128,384]{2,1,0:T(8,128)(2,1)S(1)} %back_first.4.refs_0_), channel_id=1, source_target_pairs={{0,64},{32,96},{64,0},{96,32},{128,192},{160,224},{192,128},{224,1... | collective-permute-start | bytes 589832 | tf_op jit(solution)/shard_map/ppermute | solution.py:330
  88.5 13.7 %collective-permute-start.20 = (bf16[2,128,384]{2,1,0:T(8,128)(2,1)S(1)}, bf16[2,128,384]{2,1,0:T(8,128)(2,1)S(1)}, u32[]{:S(2)}, u32[]{:S(2)}) collective-permute-start(bf16[2,128,384]{2,1,0:T(8,128)(2,1)S(1)} %back_second.7.refs_0_), channel_id=1, source_target_pairs={{0,192},{32,224},{64,128},{96,160},{128,64},{160,96},{192,0},{224,... | collective-permute-start | bytes 589832 | tf_op jit(solution)/shard_map/ppermute | solution.py:330
  98.2 9.5 %collective-permute-start.24 = (bf16[2,128,384]{2,1,0:T(8,128)(2,1)S(1)}, bf16[2,128,384]{2,1,0:T(8,128)(2,1)S(1)}, u32[]{:S(2)}, u32[]{:S(2)}) collective-permute-start(bf16[2,128,384]{2,1,0:T(8,128)(2,1)S(1)} %back_first.5.refs_0_), channel_id=1, source_target_pairs={{0,64},{32,96},{64,0},{96,32},{128,192},{160,224},{192,128},{224,1... | collective-permute-start | bytes 589832 | tf_op jit(solution)/shard_map/ppermute | solution.py:330
  98.3 9.9 %collective-permute-start.25 = (bf16[2,128,384]{2,1,0:T(8,128)(2,1)S(1)}, bf16[2,128,384]{2,1,0:T(8,128)(2,1)S(1)}, u32[]{:S(2)}, u32[]{:S(2)}) collective-permute-start(bf16[2,128,384]{2,1,0:T(8,128)(2,1)S(1)} %back_second.5.refs_0_), channel_id=1, source_target_pairs={{0,192},{32,224},{64,128},{96,160},{128,64},{160,96},{192,0},{224,... | collective-permute-start | bytes 589832 | tf_op jit(solution)/shard_map/ppermute | solution.py:330
  102.4 13.5 %collective-permute-start.23 = (bf16[2,128,384]{2,1,0:T(8,128)(2,1)S(1)}, bf16[2,128,384]{2,1,0:T(8,128)(2,1)S(1)}, u32[]{:S(2)}, u32[]{:S(2)}) collective-permute-start(bf16[2,128,384]{2,1,0:T(8,128)(2,1)S(1)} %back_first.6.refs_2_), channel_id=1, source_target_pairs={{0,64},{32,96},{64,0},{96,32},{128,192},{160,224},{192,128},{224,1... | collective-permute-start | bytes 589832 | tf_op jit(solution)/shard_map/ppermute | solution.py:330
  108.5 18.7 %collective-permute-start.26 = (bf16[2,128,384]{2,1,0:T(8,128)(2,1)S(1)}, bf16[2,128,384]{2,1,0:T(8,128)(2,1)S(1)}, u32[]{:S(2)}, u32[]{:S(2)}) collective-permute-start(bf16[2,128,384]{2,1,0:T(8,128)(2,1)S(1)} %back_first.7.refs_2_), channel_id=1, source_target_pairs={{0,64},{32,96},{64,0},{96,32},{128,192},{160,224},{192,128},{224,1... | collective-permute-start | bytes 589832 | tf_op jit(solution)/shard_map/ppermute | solution.py:330
  127.6 3.8 %collective-permute-start.27 = (bf16[2,128,1536]{2,1,0:T(8,128)(2,1)S(1)}, bf16[2,128,1536]{2,1,0:T(8,128)(2,1)S(1)}, u32[]{:S(2)}, u32[]{:S(2)}) collective-permute-start(bf16[2,128,1536]{2,1,0:T(8,128)(2,1)S(1)} %get-tuple-element.98), channel_id=1, source_target_pairs={{0,32},{32,0},{64,96},{96,64},{128,160},{160,128},{192,224},{224,1... | collective-permute-start | bytes 2359304 | tf_op jit(solution)/shard_map/ppermute | solution.py:326
where the time goes:
time: 133 us
  waiting for transfers between devices  64.1 us (48%)
  starting transfers between devices  46.3 us (35%)
  Pallas kernels  18.9 us (14%)
  local copies, waits for them, and re-layouts  2.28 us (2%)
    ppermute x16, waiting for transfers between devices, swap_fine(): lax.ppermute(block, 'fine', [(i, i ^ mask) for i in range(lax.axis_size('...  54.3 us
    ppermute x16, starting transfers between devices, swap_fine(): lax.ppermute(block, 'fine', [(i, i ^ mask) for i in range(lax.axis_size('...  29.2 us
    pallas_call x4, Pallas kernels, attend(): pl.pallas_call(functools.partial(attend_kernel, start, heads), in_specs=[...  11 us
    ppermute x8, starting transfers between devices, swap_next(): return lax.ppermute(block, ('fine', 'coarse'), route)  9.04 us
    ppermute x4, starting transfers between devices, swap_core(): lax.ppermute(block, 'fine', [(i, i ^ 1) for i in range(lax.axis_size('fin...  7.97 us
    ppermute x8, waiting for transfers between devices, swap_next(): return lax.ppermute(block, ('fine', 'coarse'), route)  7.37 us
    pallas_call x16, Pallas kernels, whole_call(): pl.pallas_call(kernel, in_specs=[pl.BlockSpec(memory_space=pltpu.VMEM)] *...  3.16 us
  transfers between devices with their start and end apart: 28, of which 15 were waited for; matrix products, arithmetic and copies ran while one was open for 0% of the time, Pallas kernels for 13%

commit v1 on v0

--- a/solution.py
+++ b/solution.py
@@ -20,9 +20,9 @@
 CHUNKS = (3, 3, 3, 3)
 PARITY = (0, 0, 0, 1)
 ORDER = (
-    "K0", "Q0", "A0", "B1", "B2", "D1", "B3", "B0", "D2", "E1",
-    "D3", "E2", "D0", "F1", "E3", "E0", "G1", "S0", "F3", "R0",
-    "F2", "F0", "G2", "H1", "G0", "H2", "G3", "H0", "T0", "H3",
+    "K0", "Q0", "A0", "B1", "B2", "D1", "B3", "D2", "B0", "E1",
+    "D3", "D0", "E2", "F1", "E3", "E0", "G1", "F2", "F3", "F0",
+    "S0", "R0", "G2", "H1", "G0", "H2", "G3", "H0", "T0", "H3",
 )
 VMEM_LIMIT = 40 * 2**20
 BF16 = jnp.bfloat16

time: 133 us -> 134 us (level)
  starting transfers between devices: 46.3 us -> 54.1 us
  waiting for transfers between devices: 64.1 us -> 57.7 us
    ppermute x8, waiting for transfers between devices: 7.37 us -> 3.42 us  [swap_next(): return lax.ppermute(block, ('fine', 'coarse'), route)]
    ppermute x8, starting transfers between devices: 9.04 us -> 12.4 us  [swap_next(): return lax.ppermute(block, ('fine', 'coarse'), route)]
    ppermute x4, starting transfers between devices: 7.97 us -> 10.5 us  [swap_core(): lax.ppermute(block, 'fine', [(i, i ^ 1) for i in range(lax.axis_size('fin...]
    ppermute x16, waiting for transfers between devices: 54.3 us -> 51.9 us  [swap_fine(): lax.ppermute(block, 'fine', [(i, i ^ mask) for i in range(lax.axis_size('...]
    ppermute x16, starting transfers between devices: 29.2 us -> 31.2 us  [swap_fine(): lax.ppermute(block, 'fine', [(i, i ^ mask) for i in range(lax.axis_size('...]
  transfers between devices with their start and end apart: 28 -> 28, of which waited for: 15 -> 13; matrix products, arithmetic and copies ran while one was open for 0% -> 0% of each run, Pallas kernels for 13% -> 13%
where the time goes in v1:
time: 134 us
  waiting for transfers between devices  57.7 us (43%)
  starting transfers between devices  54.1 us (40%)
  Pallas kernels  18.9 us (14%)
  local copies, waits for them, and re-layouts  2.28 us (2%)
    ppermute x16, waiting for transfers between devices, swap_fine(): lax.ppermute(block, 'fine', [(i, i ^ mask) for i in range(lax.axis_size('...  51.9 us
    ppermute x16, starting transfers between devices, swap_fine(): lax.ppermute(block, 'fine', [(i, i ^ mask) for i in range(lax.axis_size('...  31.2 us
    ppermute x8, starting transfers between devices, swap_next(): return lax.ppermute(block, ('fine', 'coarse'), route)  12.4 us
    pallas_call x4, Pallas kernels, attend(): pl.pallas_call(functools.partial(attend_kernel, start, heads), in_specs=[...  11 us
    ppermute x4, starting transfers between devices, swap_core(): lax.ppermute(block, 'fine', [(i, i ^ 1) for i in range(lax.axis_size('fin...  10.5 us
    ppermute x8, waiting for transfers between devices, swap_next(): return lax.ppermute(block, ('fine', 'coarse'), route)  3.42 us
    pallas_call x16, Pallas kernels, whole_call(): pl.pallas_call(kernel, in_specs=[pl.BlockSpec(memory_space=pltpu.VMEM)] *...  3.15 us
  transfers between devices with their start and end apart: 28, of which 13 were waited for; matrix products, arithmetic and copies ran while one was open for 0% of the time, Pallas kernels for 13%

profile of v1, /device:TPU:1, one launch (start us, length us, event | category | flops | bytes accessed | tf_op | source)
XLA Modules:
  0.0 134.0 jit_solution(4635480667155660629)
XLA Ops:
  0.7 1.1 copy-done
  1.8 1.1 copy-done.2
  3.0 3.3 %collective-permute-start.1 = (bf16[2,128,1536]{2,1,0:T(8,128)(2,1)S(1)}, bf16[2,128,1536]{2,1,0:T(8,128)(2,1)S(1)}, u32[]{:S(2)}, u32[]{:S(2)}) collective-permute-start(bf16[2,128,1536]{2,1,0:T(8,128)(2,1)S(1)} %extract_other.2.refs_0_), channel_id=1, source_target_pairs={{0,32},{32,0},{64,96},{96,64},{128,160},{160,128},{192,224},{224,1... | collective-permute-start | bytes 2359304 | tf_op jit(solution)/shard_map/ppermute | solution.py:326
  6.4 1.3 collective-permute-start
  7.7 0.5 collective-permute-done.1.kv_ref.refs_1_
  8.2 0.6 pack_first.1
  8.9 1.3 %collective-permute-start.4 = (bf16[2,128,384]{2,1,0:T(8,128)(2,1)S(1)}, bf16[2,128,384]{2,1,0:T(8,128)(2,1)S(1)}, u32[]{:S(2)}, u32[]{:S(2)}) collective-permute-start(bf16[2,128,384]{2,1,0:T(8,128)(2,1)S(1)} %get-tuple-element.58), channel_id=1, source_target_pairs={{0,64},{32,96},{64,0},{96,32},{128,192},{160,224},{192,128},{224,1... | collective-permute-start | bytes 589832 | tf_op jit(solution)/shard_map/ppermute | solution.py:330
  10.2 1.1 collective-permute-start.3
  11.3 13.5 %collective-permute-done.4.first_ref.refs_2_ = bf16[2,128,384]{2,1,0:T(8,128)(2,1)S(1)} collective-permute-done((bf16[2,128,384]{2,1,0:T(8,128)(2,1)S(1)}, bf16[2,128,384]{2,1,0:T(8,128)(2,1)S(1)}, u32[]{:S(2)}, u32[]{:S(2)}) %collective-permute-start.4) | collective-permute-done | bytes 196640 | tf_op jit(solution)/shard_map/ppermute | solution.py:330
  25.0 2.3 %collective-permute-start.7 = (bf16[2,128,384]{2,1,0:T(8,128)(2,1)S(1)}, bf16[2,128,384]{2,1,0:T(8,128)(2,1)S(1)}, u32[]{:S(2)}, u32[]{:S(2)}) collective-permute-start(bf16[2,128,384]{2,1,0:T(8,128)(2,1)S(1)} %pack_second.4.refs_0_), channel_id=1, source_target_pairs={{0,192},{32,224},{64,128},{96,160},{128,64},{160,96},{192,0},{224,... | collective-permute-start | bytes 589832 | tf_op jit(solution)/shard_map/ppermute | solution.py:330
  27.3 3.1 %collective-permute-start.6 = (bf16[2,128,384]{2,1,0:T(8,128)(2,1)S(1)}, bf16[2,128,384]{2,1,0:T(8,128)(2,1)S(1)}, u32[]{:S(2)}, u32[]{:S(2)}) collective-permute-start(bf16[2,128,384]{2,1,0:T(8,128)(2,1)S(1)} %get-tuple-element.60), channel_id=1, source_target_pairs={{0,64},{32,96},{64,0},{96,32},{128,192},{160,224},{192,128},{224,1... | collective-permute-start | bytes 589832 | tf_op jit(solution)/shard_map/ppermute | solution.py:330
  30.5 0.9 collective-permute-start.5
  31.5 3.1 %collective-permute-start.2 = (bf16[2,128,384]{2,1,0:T(8,128)(2,1)S(1)}, bf16[2,128,384]{2,1,0:T(8,128)(2,1)S(1)}, u32[]{:S(2)}, u32[]{:S(2)}) collective-permute-start(bf16[2,128,384]{2,1,0:T(8,128)(2,1)S(1)} %get-tuple-element.53.refs_0_), channel_id=1, source_target_pairs={{0,64},{32,96},{64,0},{96,32},{128,192},{160,224},{192,128},{224,1... | collective-permute-start | bytes 589832 | tf_op jit(solution)/shard_map/ppermute | solution.py:330
  34.6 10.0 %collective-permute-done.7.second_ref.refs_3_ = bf16[2,128,384]{2,1,0:T(8,128)(2,1)S(1)} collective-permute-done((bf16[2,128,384]{2,1,0:T(8,128)(2,1)S(1)}, bf16[2,128,384]{2,1,0:T(8,128)(2,1)S(1)}, u32[]{:S(2)}, u32[]{:S(2)}) %collective-permute-start.7) | collective-permute-done | bytes 196640 | tf_op jit(solution)/shard_map/ppermute | solution.py:330
  45.0 2.1 %collective-permute-start.9 = (bf16[2,128,384]{2,1,0:T(8,128)(2,1)S(1)}, bf16[2,128,384]{2,1,0:T(8,128)(2,1)S(1)}, u32[]{:S(2)}, u32[]{:S(2)}) collective-permute-start(bf16[2,128,384]{2,1,0:T(8,128)(2,1)S(1)} %pack_second.6.refs_0_), channel_id=1, source_target_pairs={{0,192},{32,224},{64,128},{96,160},{128,64},{160,96},{192,0},{224,... | collective-permute-start | bytes 589832 | tf_op jit(solution)/shard_map/ppermute | solution.py:330
  47.1 1.8 %collective-permute-done.5.second_ref.refs_3_ = bf16[2,128,384]{2,1,0:T(8,128)(2,1)S(1)} collective-permute-done((bf16[2,128,384]{2,1,0:T(8,128)(2,1)S(1)}, bf16[2,128,384]{2,1,0:T(8,128)(2,1)S(1)}, u32[]{:S(2)}, u32[]{:S(2)}) %collective-permute-start.5) | collective-permute-done | bytes 196640 | tf_op jit(solution)/shard_map/ppermute | solution.py:330
  49.4 1.8 %collective-permute-start.13 = (bf16[2,128,384]{2,1,0:T(8,128)(2,1)S(1)}, bf16[2,128,384]{2,1,0:T(8,128)(2,1)S(1)}, u32[]{:S(2)}, u32[]{:S(2)}) collective-permute-start(bf16[2,128,384]{2,1,0:T(8,128)(2,1)S(1)} %pack_third.5.refs_0_), channel_id=1, source_target_pairs={{0,1},{1,0},{2,3},{3,2},{4,5},{5,4},{6,7},{7,6},{8,9},{9,8},{10,11... | collective-permute-start | bytes 589832 | tf_op jit(solution)/shard_map/ppermute | solution.py:344
  51.3 2.0 %collective-permute-done.10.refs_4_ = bf16[2,128,384]{2,1,0:T(8,128)(2,1)S(1)} collective-permute-done((bf16[2,128,384]{2,1,0:T(8,128)(2,1)S(1)}, bf16[2,128,384]{2,1,0:T(8,128)(2,1)S(1)}, u32[]{:S(2)}, u32[]{:S(2)}) %collective-permute-start.10) | collective-permute-done | bytes 196640 | tf_op jit(solution)/shard_map/ppermute | solution.py:344
  53.3 2.8 %attend.4 = (bf16[2,128,1536]{2,1,0:T(8,128)(2,1)S(1)}, bf16[2,128,1536]{2,1,0:T(8,128)(2,1)S(1)}, f32[2,256,384]{2,1,0:T(8,128)S(1)}, f32[2,128,384]{2,1,0:T(8,...) custom-call(s32[1]{0:T(128)} %bitcast.core, bf16[128,3072]{1,0:T(8,128)(2,1)S(1)} %bitcast.22, ...), custom_call_target="tpu_custom_call" | custom-call | flops 1 | bytes 1 | tf_op jit(solution)/shard_map/attend/pallas_call | solution.py:208
  56.0 2.7 %collective-permute-start.14 = (bf16[2,128,384]{2,1,0:T(8,128)(2,1)S(1)}, bf16[2,128,384]{2,1,0:T(8,128)(2,1)S(1)}, u32[]{:S(2)}, u32[]{:S(2)}) collective-permute-start(bf16[2,128,384]{2,1,0:T(8,128)(2,1)S(1)} %get-tuple-element.61.refs_0_), channel_id=1, source_target_pairs={{0,1},{1,0},{2,3},{3,2},{4,5},{5,4},{6,7},{7,6},{8,9},{9,8},{10,11... | collective-permute-start | bytes 589832 | tf_op jit(solution)/shard_map/ppermute | solution.py:344
  59.1 3.4 %collective-permute-done.8.second_ref.refs_3_ = bf16[2,128,384]{2,1,0:T(8,128)(2,1)S(1)} collective-permute-done((bf16[2,128,384]{2,1,0:T(8,128)(2,1)S(1)}, bf16[2,128,384]{2,1,0:T(8,128)(2,1)S(1)}, u32[]{:S(2)}, u32[]{:S(2)}) %collective-permute-start.8) | collective-permute-done | bytes 196640 | tf_op jit(solution)/shard_map/ppermute | solution.py:330
  62.7 4.7 %collective-permute-start.11 = (bf16[2,128,384]{2,1,0:T(8,128)(2,1)S(1)}, bf16[2,128,384]{2,1,0:T(8,128)(2,1)S(1)}, u32[]{:S(2)}, u32[]{:S(2)}) collective-permute-start(bf16[2,128,384]{2,1,0:T(8,128)(2,1)S(1)} %pack_third.7.refs_7_), channel_id=1, source_target_pairs={{0,1},{1,0},{2,3},{3,2},{4,5},{5,4},{6,7},{7,6},{8,9},{9,8},{10,11... | collective-permute-start | bytes 589832 | tf_op jit(solution)/shard_map/ppermute | solution.py:344
  67.4 2.7 %attend.5 = (bf16[2,128,1536]{2,1,0:T(8,128)(2,1)S(1)}, bf16[2,128,1536]{2,1,0:T(8,128)(2,1)S(1)}, f32[2,256,384]{2,1,0:T(8,128)S(1)}, f32[2,128,384]{2,1,0:T(8,...) custom-call(s32[1]{0:T(128)} %bitcast.core, ...), custom_call_target="tpu_custom_call", output_to_operand_aliasing={{0}: (10, {}), {1}: (11, {})} | custom-call | flops 1 | bytes 1 | tf_op jit(solution)/shard_map/attend/pallas_call | solution.py:208
  70.5 1.7 %collective-permute-start.18 = (bf16[2,128,384]{2,1,0:T(8,128)(2,1)S(1)}, bf16[2,128,384]{2,1,0:T(8,128)(2,1)S(1)}, u32[]{:S(2)}, u32[]{:S(2)}) collective-permute-start(bf16[2,128,384]{2,1,0:T(8,128)(2,1)S(1)} %get-tuple-element.67.refs_0_), channel_id=1, source_target_pairs={{0,1},{1,0},{2,3},{3,2},{4,5},{5,4},{6,7},{7,6},{8,9},{9,8},{10,11... | collective-permute-start | bytes 589832 | tf_op jit(solution)/shard_map/ppermute | solution.py:344
  72.2 2.7 %attend.6 = (bf16[2,128,1536]{2,1,0:T(8,128)(2,1)S(1)}, bf16[2,128,1536]{2,1,0:T(8,128)(2,1)S(1)}, f32[2,256,384]{2,1,0:T(8,128)S(1)}, f32[2,128,384]{2,1,0:T(8,...) custom-call(s32[1]{0:T(128)} %bitcast.core, ...), custom_call_target="tpu_custom_call", output_to_operand_aliasing={{0}: (10, {}), {1}: (11, {})} | custom-call | flops 1 | bytes 1 | tf_op jit(solution)/shard_map/attend/pallas_call | solution.py:208
  75.0 2.8 %attend.7 = (bf16[2,128,1536]{2,1,0:T(8,128)(2,1)S(1)}, bf16[2,128,1536]{2,1,0:T(8,128)(2,1)S(1)}, f32[2,256,384]{2,1,0:T(8,128)S(1)}, f32[2,128,384]{2,1,0:T(8,...) custom-call(s32[1]{0:T(128)} %bitcast.core, ...), custom_call_target="tpu_custom_call", output_to_operand_aliasing={{0}: (10, {}), {1}: (11, {})} | custom-call | flops 1 | bytes 1 | tf_op jit(solution)/shard_map/attend/pallas_call | solution.py:208
  77.7 5.2 %collective-permute-start.15 = (bf16[2,128,1536]{2,1,0:T(8,128)(2,1)S(1)}, bf16[2,128,1536]{2,1,0:T(8,128)(2,1)S(1)}, u32[]{:S(2)}, u32[]{:S(2)}) collective-permute-start(bf16[2,128,1536]{2,1,0:T(8,128)(2,1)S(1)} %get-tuple-element.72), channel_id=1, source_target_pairs={{0,32},{32,0},{64,96},{96,64},{128,160},{160,128},{192,224},{224,1... | collective-permute-start | bytes 2359304 | tf_op jit(solution)/shard_map/ppermute | solution.py:326
  83.0 1.2 collective-permute-start.17
  84.6 2.8 %collective-permute-start.22 = (bf16[2,128,384]{2,1,0:T(8,128)(2,1)S(1)}, bf16[2,128,384]{2,1,0:T(8,128)(2,1)S(1)}, u32[]{:S(2)}, u32[]{:S(2)}) collective-permute-start(bf16[2,128,384]{2,1,0:T(8,128)(2,1)S(1)} %back_second.5.refs_0_), channel_id=1, source_target_pairs={{0,192},{32,224},{64,128},{96,160},{128,64},{160,96},{192,0},{224,... | collective-permute-start | bytes 589832 | tf_op jit(solution)/shard_map/ppermute | solution.py:330
  87.4 1.9 %collective-permute-start.21 = (bf16[2,128,384]{2,1,0:T(8,128)(2,1)S(1)}, bf16[2,128,384]{2,1,0:T(8,128)(2,1)S(1)}, u32[]{:S(2)}, u32[]{:S(2)}) collective-permute-start(bf16[2,128,384]{2,1,0:T(8,128)(2,1)S(1)} %back_first.4.refs_0_), channel_id=1, source_target_pairs={{0,64},{32,96},{64,0},{96,32},{128,192},{160,224},{192,128},{224,1... | collective-permute-start | bytes 589832 | tf_op jit(solution)/shard_map/ppermute | solution.py:330
  89.2 1.4 %collective-permute-done.17.third_ref = bf16[2,128,384]{2,1,0:T(8,128)(2,1)S(1)} collective-permute-done((bf16[2,128,384]{2,1,0:T(8,128)(2,1)S(1)}, bf16[2,128,384]{2,1,0:T(8,128)(2,1)S(1)}, u32[]{:S(2)}, u32[]{:S(2)}) %collective-permute-start.17) | collective-permute-done | bytes 196640 | tf_op jit(solution)/shard_map/ppermute | solution.py:344
  91.0 1.9 %collective-permute-start.20 = (bf16[2,128,384]{2,1,0:T(8,128)(2,1)S(1)}, bf16[2,128,384]{2,1,0:T(8,128)(2,1)S(1)}, u32[]{:S(2)}, u32[]{:S(2)}) collective-permute-start(bf16[2,128,384]{2,1,0:T(8,128)(2,1)S(1)} %back_second.7.refs_0_), channel_id=1, source_target_pairs={{0,192},{32,224},{64,128},{96,160},{128,64},{160,96},{192,0},{224,... | collective-permute-start | bytes 589832 | tf_op jit(solution)/shard_map/ppermute | solution.py:330
  93.0 7.0 %collective-permute-done.22.second_ref = bf16[2,128,384]{2,1,0:T(8,128)(2,1)S(1)} collective-permute-done((bf16[2,128,384]{2,1,0:T(8,128)(2,1)S(1)}, bf16[2,128,384]{2,1,0:T(8,128)(2,1)S(1)}, u32[]{:S(2)}, u32[]{:S(2)}) %collective-permute-start.22) | collective-permute-done | bytes 196640 | tf_op jit(solution)/shard_map/ppermute | solution.py:330
  100.3 2.7 %collective-permute-start.25 = (bf16[2,128,384]{2,1,0:T(8,128)(2,1)S(1)}, bf16[2,128,384]{2,1,0:T(8,128)(2,1)S(1)}, u32[]{:S(2)}, u32[]{:S(2)}) collective-permute-start(bf16[2,128,384]{2,1,0:T(8,128)(2,1)S(1)} %back_second.6.refs_0_), channel_id=1, source_target_pairs={{0,192},{32,224},{64,128},{96,160},{128,64},{160,96},{192,0},{224,... | collective-permute-start | bytes 589832 | tf_op jit(solution)/shard_map/ppermute | solution.py:330
  103.0 0.4 finish.4
  103.5 4.2 %collective-permute-done.20.second_ref = bf16[2,128,384]{2,1,0:T(8,128)(2,1)S(1)} collective-permute-done((bf16[2,128,384]{2,1,0:T(8,128)(2,1)S(1)}, bf16[2,128,384]{2,1,0:T(8,128)(2,1)S(1)}, u32[]{:S(2)}, u32[]{:S(2)}) %collective-permute-start.20) | collective-permute-done | bytes 196640 | tf_op jit(solution)/shard_map/ppermute | solution.py:330
  107.9 3.7 %collective-permute-start.23 = (bf16[2,128,384]{2,1,0:T(8,128)(2,1)S(1)}, bf16[2,128,384]{2,1,0:T(8,128)(2,1)S(1)}, u32[]{:S(2)}, u32[]{:S(2)}) collective-permute-start(bf16[2,128,384]{2,1,0:T(8,128)(2,1)S(1)} %back_first.6.refs_2_), channel_id=1, source_target_pairs={{0,64},{32,96},{64,0},{96,32},{128,192},{160,224},{192,128},{224,1... | collective-permute-start | bytes 589832 | tf_op jit(solution)/shard_map/ppermute | solution.py:330
  111.5 0.4 finish.5
  111.9 0.8 collective-permute-done.25.second_ref
  113.0 4.0 %collective-permute-start.26 = (bf16[2,128,384]{2,1,0:T(8,128)(2,1)S(1)}, bf16[2,128,384]{2,1,0:T(8,128)(2,1)S(1)}, u32[]{:S(2)}, u32[]{:S(2)}) collective-permute-start(bf16[2,128,384]{2,1,0:T(8,128)(2,1)S(1)} %back_first.7.refs_2_), channel_id=1, source_target_pairs={{0,64},{32,96},{64,0},{96,32},{128,192},{160,224},{192,128},{224,1... | collective-permute-start | bytes 589832 | tf_op jit(solution)/shard_map/ppermute | solution.py:330
  117.0 0.9 collective-permute-done.23.first_ref
  117.8 0.4 finish.6
  118.2 1.2 assemble.2
  119.5 10.3 %collective-permute-done.26.first_ref = bf16[2,128,384]{2,1,0:T(8,128)(2,1)S(1)} collective-permute-done((bf16[2,128,384]{2,1,0:T(8,128)(2,1)S(1)}, bf16[2,128,384]{2,1,0:T(8,128)(2,1)S(1)}, u32[]{:S(2)}, u32[]{:S(2)}) %collective-permute-start.26) | collective-permute-done | bytes 196640 | tf_op jit(solution)/shard_map/ppermute | solution.py:330
  129.8 0.4 finish.7
  130.2 0.7 collective-permute-start.27
  130.9 1.9 %collective-permute-done.27.recv_ref = bf16[2,128,1536]{2,1,0:T(8,128)(2,1)S(1)} collective-permute-done((bf16[2,128,1536]{2,1,0:T(8,128)(2,1)S(1)}, bf16[2,128,1536]{2,1,0:T(8,128)(2,1)S(1)}, u32[]{:S(2)}, u32[]{:S(2)}) %collective-permute-start.27) | collective-permute-done | bytes 786464 | tf_op jit(solution)/shard_map/ppermute | solution.py:326
  132.8 1.2 assemble.3
  (49 shorter events, 3.8 us)
Async XLA Ops:
  0.6 1.1 copy-start
  1.8 1.1 copy-start.2
  2.9 3.4 %copy-start.4 = (bf16[1,1,128,3072]{3,2,1,0:T(8,128)(2,1)S(1)}, bf16[1,1,128,3072]{3,2,1,0:T(8,128)(2,1)}, u32[]{:S(2)}) copy-start(bf16[1,1,128,3072]{3,2,1,0:T(8,128)(2,1)} %param.4) | copy-start | bytes 2359300
  2.9 3.4 %copy-start.5 = (bf16[1,1,128,3072]{3,2,1,0:T(8,128)(2,1)S(1)}, bf16[1,1,128,3072]{3,2,1,0:T(8,128)(2,1)}, u32[]{:S(2)}) copy-start(bf16[1,1,128,3072]{3,2,1,0:T(8,128)(2,1)} %param.7) | copy-start | bytes 2359300
  3.0 5.2 %collective-permute-start.1 = (bf16[2,128,1536]{2,1,0:T(8,128)(2,1)S(1)}, bf16[2,128,1536]{2,1,0:T(8,128)(2,1)S(1)}, u32[]{:S(2)}, u32[]{:S(2)}) collective-permute-start(bf16[2,128,1536]{2,1,0:T(8,128)(2,1)S(1)} %extract_other.2.refs_0_), channel_id=1, source_target_pairs={{0,32},{32,0},{64,96},{96,64},{128,160},{160,128},{192,224},{224,1... | collective-permute-start | bytes 2359304 | tf_op jit(solution)/shard_map/ppermute | solution.py:326
  6.3 1.9 %copy-start.1 = (bf16[1,1,128,3072]{3,2,1,0:T(8,128)(2,1)S(1)}, bf16[1,1,128,3072]{3,2,1,0:T(8,128)(2,1)}, u32[]{:S(2)}) copy-start(bf16[1,1,128,3072]{3,2,1,0:T(8,128)(2,1)} %param.5) | copy-start | bytes 2359300
  6.3 1.9 %copy-start.3 = (bf16[1,1,128,3072]{3,2,1,0:T(8,128)(2,1)S(1)}, bf16[1,1,128,3072]{3,2,1,0:T(8,128)(2,1)}, u32[]{:S(2)}) copy-start(bf16[1,1,128,3072]{3,2,1,0:T(8,128)(2,1)} %param.6) | copy-start | bytes 2359300
  6.4 44.9 %collective-permute-start = (bf16[2,128,1536]{2,1,0:T(8,128)(2,1)S(1)}, bf16[2,128,1536]{2,1,0:T(8,128)(2,1)S(1)}, u32[]{:S(2)}, u32[]{:S(2)}) collective-permute-start(bf16[2,128,1536]{2,1,0:T(8,128)(2,1)S(1)} %extract_other.3.refs_0_), channel_id=1, source_target_pairs={{0,32},{32,0},{64,96},{96,64},{128,160},{160,128},{192,224},{224,1... | collective-permute-start | bytes 2359304 | tf_op jit(solution)/shard_map/ppermute | solution.py:326
  8.9 16.0 %collective-permute-start.4 = (bf16[2,128,384]{2,1,0:T(8,128)(2,1)S(1)}, bf16[2,128,384]{2,1,0:T(8,128)(2,1)S(1)}, u32[]{:S(2)}, u32[]{:S(2)}) collective-permute-start(bf16[2,128,384]{2,1,0:T(8,128)(2,1)S(1)} %get-tuple-element.58), channel_id=1, source_target_pairs={{0,64},{32,96},{64,0},{96,32},{128,192},{160,224},{192,128},{224,1... | collective-permute-start | bytes 589832 | tf_op jit(solution)/shard_map/ppermute | solution.py:330
  10.2 20.2 %collective-permute-start.3 = (bf16[2,128,384]{2,1,0:T(8,128)(2,1)S(1)}, bf16[2,128,384]{2,1,0:T(8,128)(2,1)S(1)}, u32[]{:S(2)}, u32[]{:S(2)}) collective-permute-start(bf16[2,128,384]{2,1,0:T(8,128)(2,1)S(1)} %get-tuple-element.56), channel_id=1, source_target_pairs={{0,64},{32,96},{64,0},{96,32},{128,192},{160,224},{192,128},{224,1... | collective-permute-start | bytes 589832 | tf_op jit(solution)/shard_map/ppermute | solution.py:330
  25.0 19.5 %collective-permute-start.7 = (bf16[2,128,384]{2,1,0:T(8,128)(2,1)S(1)}, bf16[2,128,384]{2,1,0:T(8,128)(2,1)S(1)}, u32[]{:S(2)}, u32[]{:S(2)}) collective-permute-start(bf16[2,128,384]{2,1,0:T(8,128)(2,1)S(1)} %pack_second.4.refs_0_), channel_id=1, source_target_pairs={{0,192},{32,224},{64,128},{96,160},{128,64},{160,96},{192,0},{224,... | collective-permute-start | bytes 589832 | tf_op jit(solution)/shard_map/ppermute | solution.py:330
  27.3 17.6 %collective-permute-start.6 = (bf16[2,128,384]{2,1,0:T(8,128)(2,1)S(1)}, bf16[2,128,384]{2,1,0:T(8,128)(2,1)S(1)}, u32[]{:S(2)}, u32[]{:S(2)}) collective-permute-start(bf16[2,128,384]{2,1,0:T(8,128)(2,1)S(1)} %get-tuple-element.60), channel_id=1, source_target_pairs={{0,64},{32,96},{64,0},{96,32},{128,192},{160,224},{192,128},{224,1... | collective-permute-start | bytes 589832 | tf_op jit(solution)/shard_map/ppermute | solution.py:330
  30.5 18.4 %collective-permute-start.5 = (bf16[2,128,384]{2,1,0:T(8,128)(2,1)S(1)}, bf16[2,128,384]{2,1,0:T(8,128)(2,1)S(1)}, u32[]{:S(2)}, u32[]{:S(2)}) collective-permute-start(bf16[2,128,384]{2,1,0:T(8,128)(2,1)S(1)} %pack_second.5.refs_0_), channel_id=1, source_target_pairs={{0,192},{32,224},{64,128},{96,160},{128,64},{160,96},{192,0},{224,... | collective-permute-start | bytes 589832 | tf_op jit(solution)/shard_map/ppermute | solution.py:330
  31.5 17.7 %collective-permute-start.2 = (bf16[2,128,384]{2,1,0:T(8,128)(2,1)S(1)}, bf16[2,128,384]{2,1,0:T(8,128)(2,1)S(1)}, u32[]{:S(2)}, u32[]{:S(2)}) collective-permute-start(bf16[2,128,384]{2,1,0:T(8,128)(2,1)S(1)} %get-tuple-element.53.refs_0_), channel_id=1, source_target_pairs={{0,64},{32,96},{64,0},{96,32},{128,192},{160,224},{192,128},{224,1... | collective-permute-start | bytes 589832 | tf_op jit(solution)/shard_map/ppermute | solution.py:330
  44.7 8.5 %collective-permute-start.10 = (bf16[2,128,384]{2,1,0:T(8,128)(2,1)S(1)}, bf16[2,128,384]{2,1,0:T(8,128)(2,1)S(1)}, u32[]{:S(2)}, u32[]{:S(2)}) collective-permute-start(bf16[2,128,384]{2,1,0:T(8,128)(2,1)S(1)} %pack_third.4.refs_0_), channel_id=1, source_target_pairs={{0,1},{1,0},{2,3},{3,2},{4,5},{5,4},{6,7},{7,6},{8,9},{9,8},{10,11... | collective-permute-start | bytes 589832 | tf_op jit(solution)/shard_map/ppermute | solution.py:344
  45.0 13.7 %collective-permute-start.9 = (bf16[2,128,384]{2,1,0:T(8,128)(2,1)S(1)}, bf16[2,128,384]{2,1,0:T(8,128)(2,1)S(1)}, u32[]{:S(2)}, u32[]{:S(2)}) collective-permute-start(bf16[2,128,384]{2,1,0:T(8,128)(2,1)S(1)} %pack_second.6.refs_0_), channel_id=1, source_target_pairs={{0,192},{32,224},{64,128},{96,160},{128,64},{160,96},{192,0},{224,... | collective-permute-start | bytes 589832 | tf_op jit(solution)/shard_map/ppermute | solution.py:330
  49.3 13.2 %collective-permute-start.8 = (bf16[2,128,384]{2,1,0:T(8,128)(2,1)S(1)}, bf16[2,128,384]{2,1,0:T(8,128)(2,1)S(1)}, u32[]{:S(2)}, u32[]{:S(2)}) collective-permute-start(bf16[2,128,384]{2,1,0:T(8,128)(2,1)S(1)} %pack_second.7.refs_5_), channel_id=1, source_target_pairs={{0,192},{32,224},{64,128},{96,160},{128,64},{160,96},{192,0},{224,... | collective-permute-start | bytes 589832 | tf_op jit(solution)/shard_map/ppermute | solution.py:330
  49.4 18.0 %collective-permute-start.13 = (bf16[2,128,384]{2,1,0:T(8,128)(2,1)S(1)}, bf16[2,128,384]{2,1,0:T(8,128)(2,1)S(1)}, u32[]{:S(2)}, u32[]{:S(2)}) collective-permute-start(bf16[2,128,384]{2,1,0:T(8,128)(2,1)S(1)} %pack_third.5.refs_0_), channel_id=1, source_target_pairs={{0,1},{1,0},{2,3},{3,2},{4,5},{5,4},{6,7},{7,6},{8,9},{9,8},{10,11... | collective-permute-start | bytes 589832 | tf_op jit(solution)/shard_map/ppermute | solution.py:344
  56.0 14.1 %collective-permute-start.14 = (bf16[2,128,384]{2,1,0:T(8,128)(2,1)S(1)}, bf16[2,128,384]{2,1,0:T(8,128)(2,1)S(1)}, u32[]{:S(2)}, u32[]{:S(2)}) collective-permute-start(bf16[2,128,384]{2,1,0:T(8,128)(2,1)S(1)} %get-tuple-element.61.refs_0_), channel_id=1, source_target_pairs={{0,1},{1,0},{2,3},{3,2},{4,5},{5,4},{6,7},{7,6},{8,9},{9,8},{10,11... | collective-permute-start | bytes 589832 | tf_op jit(solution)/shard_map/ppermute | solution.py:344
  59.0 13.3 %collective-permute-start.12 = (bf16[2,128,384]{2,1,0:T(8,128)(2,1)S(1)}, bf16[2,128,384]{2,1,0:T(8,128)(2,1)S(1)}, u32[]{:S(2)}, u32[]{:S(2)}) collective-permute-start(bf16[2,128,384]{2,1,0:T(8,128)(2,1)S(1)} %pack_third.6.refs_0_), channel_id=1, source_target_pairs={{0,193},{1,64},{2,195},{3,66},{4,197},{5,68},{6,199},{7,70},{8,201... | collective-permute-start | bytes 589832 | tf_op jit(solution)/shard_map/ppermute | solution.py:344
  62.7 12.3 %collective-permute-start.11 = (bf16[2,128,384]{2,1,0:T(8,128)(2,1)S(1)}, bf16[2,128,384]{2,1,0:T(8,128)(2,1)S(1)}, u32[]{:S(2)}, u32[]{:S(2)}) collective-permute-start(bf16[2,128,384]{2,1,0:T(8,128)(2,1)S(1)} %pack_third.7.refs_7_), channel_id=1, source_target_pairs={{0,1},{1,0},{2,3},{3,2},{4,5},{5,4},{6,7},{7,6},{8,9},{9,8},{10,11... | collective-permute-start | bytes 589832 | tf_op jit(solution)/shard_map/ppermute | solution.py:344
  70.4 13.8 %collective-permute-start.19 = (bf16[2,128,384]{2,1,0:T(8,128)(2,1)S(1)}, bf16[2,128,384]{2,1,0:T(8,128)(2,1)S(1)}, u32[]{:S(2)}, u32[]{:S(2)}) collective-permute-start(bf16[2,128,384]{2,1,0:T(8,128)(2,1)S(1)} %back_second.4.refs_7_), channel_id=1, source_target_pairs={{0,192},{32,224},{64,128},{96,160},{128,64},{160,96},{192,0},{224,... | collective-permute-start | bytes 589832 | tf_op jit(solution)/shard_map/ppermute | solution.py:330
  70.5 13.9 %collective-permute-start.18 = (bf16[2,128,384]{2,1,0:T(8,128)(2,1)S(1)}, bf16[2,128,384]{2,1,0:T(8,128)(2,1)S(1)}, u32[]{:S(2)}, u32[]{:S(2)}) collective-permute-start(bf16[2,128,384]{2,1,0:T(8,128)(2,1)S(1)} %get-tuple-element.67.refs_0_), channel_id=1, source_target_pairs={{0,1},{1,0},{2,3},{3,2},{4,5},{5,4},{6,7},{7,6},{8,9},{9,8},{10,11... | collective-permute-start | bytes 589832 | tf_op jit(solution)/shard_map/ppermute | solution.py:344
  77.7 40.5 %collective-permute-start.15 = (bf16[2,128,1536]{2,1,0:T(8,128)(2,1)S(1)}, bf16[2,128,1536]{2,1,0:T(8,128)(2,1)S(1)}, u32[]{:S(2)}, u32[]{:S(2)}) collective-permute-start(bf16[2,128,1536]{2,1,0:T(8,128)(2,1)S(1)} %get-tuple-element.72), channel_id=1, source_target_pairs={{0,32},{32,0},{64,96},{96,64},{128,160},{160,128},{192,224},{224,1... | collective-permute-start | bytes 2359304 | tf_op jit(solution)/shard_map/ppermute | solution.py:326
  83.0 7.7 %collective-permute-start.17 = (bf16[2,128,384]{2,1,0:T(8,128)(2,1)S(1)}, bf16[2,128,384]{2,1,0:T(8,128)(2,1)S(1)}, u32[]{:S(2)}, u32[]{:S(2)}) collective-permute-start(bf16[2,128,384]{2,1,0:T(8,128)(2,1)S(1)} %get-tuple-element.70.refs_7_), channel_id=1, source_target_pairs={{0,193},{1,64},{2,195},{3,66},{4,197},{5,68},{6,199},{7,70},{8,201... | collective-permute-start | bytes 589832 | tf_op jit(solution)/shard_map/ppermute | solution.py:344
  84.1 6.7 %collective-permute-start.16 = (bf16[2,128,384]{2,1,0:T(8,128)(2,1)S(1)}, bf16[2,128,384]{2,1,0:T(8,128)(2,1)S(1)}, u32[]{:S(2)}, u32[]{:S(2)}) collective-permute-start(bf16[2,128,384]{2,1,0:T(8,128)(2,1)S(1)} %get-tuple-element.76.refs_0_), channel_id=1, source_target_pairs={{0,1},{1,0},{2,3},{3,2},{4,5},{5,4},{6,7},{7,6},{8,9},{9,8},{10,11... | collective-permute-start | bytes 589832 | tf_op jit(solution)/shard_map/ppermute | solution.py:344
  84.6 15.4 %collective-permute-start.22 = (bf16[2,128,384]{2,1,0:T(8,128)(2,1)S(1)}, bf16[2,128,384]{2,1,0:T(8,128)(2,1)S(1)}, u32[]{:S(2)}, u32[]{:S(2)}) collective-permute-start(bf16[2,128,384]{2,1,0:T(8,128)(2,1)S(1)} %back_second.5.refs_0_), channel_id=1, source_target_pairs={{0,192},{32,224},{64,128},{96,160},{128,64},{160,96},{192,0},{224,... | collective-permute-start | bytes 589832 | tf_op jit(solution)/shard_map/ppermute | solution.py:330
  87.4 15.7 %collective-permute-start.21 = (bf16[2,128,384]{2,1,0:T(8,128)(2,1)S(1)}, bf16[2,128,384]{2,1,0:T(8,128)(2,1)S(1)}, u32[]{:S(2)}, u32[]{:S(2)}) collective-permute-start(bf16[2,128,384]{2,1,0:T(8,128)(2,1)S(1)} %back_first.4.refs_0_), channel_id=1, source_target_pairs={{0,64},{32,96},{64,0},{96,32},{128,192},{160,224},{192,128},{224,1... | collective-permute-start | bytes 589832 | tf_op jit(solution)/shard_map/ppermute | solution.py:330
  91.0 16.6 %collective-permute-start.20 = (bf16[2,128,384]{2,1,0:T(8,128)(2,1)S(1)}, bf16[2,128,384]{2,1,0:T(8,128)(2,1)S(1)}, u32[]{:S(2)}, u32[]{:S(2)}) collective-permute-start(bf16[2,128,384]{2,1,0:T(8,128)(2,1)S(1)} %back_second.7.refs_0_), channel_id=1, source_target_pairs={{0,192},{32,224},{64,128},{96,160},{128,64},{160,96},{192,0},{224,... | collective-permute-start | bytes 589832 | tf_op jit(solution)/shard_map/ppermute | solution.py:330
  100.2 11.3 %collective-permute-start.24 = (bf16[2,128,384]{2,1,0:T(8,128)(2,1)S(1)}, bf16[2,128,384]{2,1,0:T(8,128)(2,1)S(1)}, u32[]{:S(2)}, u32[]{:S(2)}) collective-permute-start(bf16[2,128,384]{2,1,0:T(8,128)(2,1)S(1)} %back_first.5.refs_0_), channel_id=1, source_target_pairs={{0,64},{32,96},{64,0},{96,32},{128,192},{160,224},{192,128},{224,1... | collective-permute-start | bytes 589832 | tf_op jit(solution)/shard_map/ppermute | solution.py:330
  100.3 12.4 %collective-permute-start.25 = (bf16[2,128,384]{2,1,0:T(8,128)(2,1)S(1)}, bf16[2,128,384]{2,1,0:T(8,128)(2,1)S(1)}, u32[]{:S(2)}, u32[]{:S(2)}) collective-permute-start(bf16[2,128,384]{2,1,0:T(8,128)(2,1)S(1)} %back_second.6.refs_0_), channel_id=1, source_target_pairs={{0,192},{32,224},{64,128},{96,160},{128,64},{160,96},{192,0},{224,... | collective-permute-start | bytes 589832 | tf_op jit(solution)/shard_map/ppermute | solution.py:330
  107.9 10.0 %collective-permute-start.23 = (bf16[2,128,384]{2,1,0:T(8,128)(2,1)S(1)}, bf16[2,128,384]{2,1,0:T(8,128)(2,1)S(1)}, u32[]{:S(2)}, u32[]{:S(2)}) collective-permute-start(bf16[2,128,384]{2,1,0:T(8,128)(2,1)S(1)} %back_first.6.refs_2_), channel_id=1, source_target_pairs={{0,64},{32,96},{64,0},{96,32},{128,192},{160,224},{192,128},{224,1... | collective-permute-start | bytes 589832 | tf_op jit(solution)/shard_map/ppermute | solution.py:330
  113.0 16.8 %collective-permute-start.26 = (bf16[2,128,384]{2,1,0:T(8,128)(2,1)S(1)}, bf16[2,128,384]{2,1,0:T(8,128)(2,1)S(1)}, u32[]{:S(2)}, u32[]{:S(2)}) collective-permute-start(bf16[2,128,384]{2,1,0:T(8,128)(2,1)S(1)} %back_first.7.refs_2_), channel_id=1, source_target_pairs={{0,64},{32,96},{64,0},{96,32},{128,192},{160,224},{192,128},{224,1... | collective-permute-start | bytes 589832 | tf_op jit(solution)/shard_map/ppermute | solution.py:330
  130.2 2.6 %collective-permute-start.27 = (bf16[2,128,1536]{2,1,0:T(8,128)(2,1)S(1)}, bf16[2,128,1536]{2,1,0:T(8,128)(2,1)S(1)}, u32[]{:S(2)}, u32[]{:S(2)}) collective-permute-start(bf16[2,128,1536]{2,1,0:T(8,128)(2,1)S(1)} %get-tuple-element.98), channel_id=1, source_target_pairs={{0,32},{32,0},{64,96},{96,64},{128,160},{160,128},{192,224},{224,1... | collective-permute-start | bytes 2359304 | tf_op jit(solution)/shard_map/ppermute | solution.py:326
